TPU v7x, 256 devices: a whole 4x4x8 slice. The times are simulated.
256 devices in a mesh: dp: 32 (over y, x, core), mp: 8 (over z).
Axes of the slice: x: 4, y: 4, z: 8, core: 2. Of those that a mesh axis runs over, the one named last changes fastest.
Arguments:
- queries: bfloat16 [65536, 4096], P('dp', 'mp'), may hold values from -5 to 5
- rotated_key_state: bfloat16 [65536, 1024], P('dp', 'mp'), may hold values from -5 to 5
- value_state_rows: bfloat16 [65536, 1024], P('dp', 'mp'), may hold values from -6 to 6
- out_weight: bfloat16 [4096, 8192], P('mp', 'dp'), may hold values from -0.375 to 0.375
- segments: int32 [65536], P('dp'), may hold values from -1 to 4, as said below
- send_plan: int32 [512], replicated, may hold values from -1 to 255, as said below
Outputs:
- projected: bfloat16 [32768, 8192], P(('dp', 'mp'))
Inputs may be any that keep to these rules, and one draw needn't show every extreme that they name: `segments`: in each group segment numbers start at 0 on the first row, never fall, and are -1 exactly on the rows of dead blocks, which follow the live ones. No response is longer than 1024 tokens; the first response of each group has 1024 tokens unless the group's live rows end before. Some group has all 16 blocks live and some group none. `send_plan`: live blocks (those with segment numbers of 0 or more) name each balanced slot exactly once, slot s meaning row block s of the balanced order and data group s // 8; dead blocks hold -1. From one group at most 1 block go to the same group, and some pair of groups reaches 1.
All inputs are finite; a program needn't handle non-finite values.
Results may differ from a plain program's by a relative error of at most 0.017.
Values may be sent and summed in bfloat16 or wider, within the bound.
No kernel may reach another device: no remote copies, remote signals or barrier semaphores. Data moves between devices by JAX's collectives and lax.ppermute only.
A program may use at most 128 MiB of HBM per device.

v0:
```python
import math

import jax
import jax.numpy as jnp
from jax import lax
from jax.sharding import PartitionSpec as P

HEAD_SIZE = 128
RESPONSE_BLOCK = 128
QUERY_BLOCK = 512
BAL = 8


def attend_block(
    query_rows,
    key_rows,
    value_rows,
    query_numbers,
    key_numbers,
    query_position,
    key_position,
    kv_heads,
    group_width,
):
    head_queries = query_rows.reshape(query_rows.shape[0], kv_heads, group_width, HEAD_SIZE)
    head_keys = key_rows.reshape(key_rows.shape[0], kv_heads, HEAD_SIZE)
    head_values = value_rows.reshape(value_rows.shape[0], kv_heads, HEAD_SIZE)
    scores = jnp.einsum(
        "qkgd,nkd->kgqn", head_queries, head_keys, preferred_element_type=jnp.float32
    ) * (1.0 / math.sqrt(HEAD_SIZE))
    allowed = (query_numbers[:, None] == key_numbers[None, :]) & (
        key_position[None, :] <= query_position[:, None]
    )
    scores = jnp.where(allowed[None, None], scores, -1e30)
    row_max = jnp.max(scores, axis=-1, keepdims=True)
    weights = jnp.exp(scores - row_max)
    row_total = jnp.sum(weights, axis=-1)
    mixture = jnp.einsum(
        "kgqn,nkd->qkgd",
        weights.astype(jnp.bfloat16),
        head_values,
        preferred_element_type=jnp.float32,
    )
    mixture = mixture / jnp.transpose(row_total, (2, 0, 1))[..., None]
    return mixture.reshape(query_rows.shape[0], query_rows.shape[1]).astype(jnp.bfloat16)


def owner_attention(queries, rotated_key_state, value_state_rows, segments):
    count_of_rows = queries.shape[0]
    kv_heads = rotated_key_state.shape[1] // HEAD_SIZE
    group_width = queries.shape[1] // HEAD_SIZE // kv_heads
    position = jnp.arange(count_of_rows)
    pieces = []
    for query_first_row in range(0, count_of_rows, QUERY_BLOCK):
        query_stop_row = query_first_row + QUERY_BLOCK
        key_start = 0
        pieces.append(
            attend_block(
                queries[query_first_row:query_stop_row],
                rotated_key_state[key_start:query_stop_row],
                value_state_rows[key_start:query_stop_row],
                segments[query_first_row:query_stop_row],
                segments[key_start:query_stop_row],
                position[query_first_row:query_stop_row],
                position[key_start:query_stop_row],
                kv_heads,
                group_width,
            )
        )
    return jnp.concatenate(pieces, axis=0)


def on_device(queries, rotated_key_state, value_state_rows, out_weight, segments, send_plan):
    count_of_rows, query_cols = queries.shape
    attended_rows = owner_attention(queries, rotated_key_state, value_state_rows, segments)
    groups = lax.axis_size("dp")
    myself = lax.axis_index("dp")
    cap_blocks = count_of_rows // RESPONSE_BLOCK
    pair_slots = (cap_blocks + groups - 1) // groups
    plan_grid = send_plan.reshape(groups, cap_blocks)
    dest_group = jnp.where(plan_grid >= 0, plan_grid // BAL, -1)
    block_ids = jnp.arange(cap_blocks)
    earlier = block_ids[None, :] < block_ids[:, None]
    same_dest = (dest_group[:, :, None] == dest_group[:, None, :]) & earlier[None]
    pair_rank = jnp.sum(same_dest.astype(jnp.int32), axis=2)
    my_dest = lax.dynamic_index_in_dim(dest_group, myself, 0, keepdims=False)
    my_rank = lax.dynamic_index_in_dim(pair_rank, myself, 0, keepdims=False)
    chosen = (my_dest[None, None, :] == jnp.arange(groups)[:, None, None]) & (
        my_rank[None, None, :] == jnp.arange(pair_slots)[None, :, None]
    )
    found = jnp.any(chosen, axis=2)
    source_block = jnp.sum(jnp.where(chosen, block_ids[None, None, :], 0), axis=2)
    source_block = jnp.where(found, source_block, cap_blocks)
    padded = jnp.concatenate(
        [
            attended_rows.reshape(cap_blocks, RESPONSE_BLOCK, query_cols),
            jnp.zeros((1, RESPONSE_BLOCK, query_cols), jnp.bfloat16),
        ],
        axis=0,
    )
    outgoing = padded[source_block]
    incoming = lax.all_to_all(outgoing, "dp", split_axis=0, concat_axis=0, tiled=True)
    wanted = myself * BAL + jnp.arange(BAL)
    matches = send_plan[None, :] == wanted[:, None]
    arrival = jnp.arange(groups * cap_blocks) // cap_blocks * pair_slots + pair_rank.reshape(-1)
    slot_source = jnp.sum(jnp.where(matches, arrival[None, :], 0), axis=1)
    placed = incoming.reshape(groups * pair_slots, RESPONSE_BLOCK, query_cols)[slot_source].reshape(
        BAL * RESPONSE_BLOCK, query_cols
    )
    partial_sums = jnp.dot(
        placed,
        lax.all_gather(out_weight, "dp", axis=1, tiled=True),
        preferred_element_type=jnp.float32,
    )
    summed = lax.psum_scatter(
        partial_sums.astype(jnp.bfloat16), "mp", scatter_dimension=0, tiled=True
    )
    return summed


def solution(mesh):
    in_specs = (P("dp", "mp"), P("dp", "mp"), P("dp", "mp"), P("mp", "dp"), P("dp"), P())
    out_specs = P(("dp", "mp"), None)
    return jax.shard_map(
        on_device, mesh=mesh, in_specs=in_specs, out_specs=out_specs, check_vma=False
    )
```

profile of v0, /device:TPU:1, one launch (start us, length us, event | category | flops | bytes accessed | tf_op | source)
XLA Modules:
  0.0 321.5 jit_solution(11274983457210147918)
XLA Ops:
  7.3 1.7 fusion.87
  10.2 0.8 compare_and_fusion.1
  11.0 0.9 fusion.24
  11.9 0.9 fusion.22
  12.8 1.3 divide_convert_fusion.3
  14.1 1.6 fusion.12
  15.7 1.0 fusion.20
  16.7 1.2 compare_and_fusion
  17.9 5.8 %fusion.5 = (f32[4,512]{1,0:T(4,128)S(1)}, f32[1536,512,4]{1,0,2:T(8,128)}) fusion(pred[512,1536]{0,1:T(8,128)(4,1)S(1)} %compare_and_fusion, bf16[512,4,128]{0,2,1:T(8,128)(2,1)S(1)} %bitcast.220, bf16[2048,128]{1,0:T(8,128)(2,1)S(1)} %copy-done), kind=kOutput, calls=%fused_computation.12 | convolution fusion | flops 814741504 | bytes 14295040 | tf_op jit(solution)/shard_map/qkgd,nkd->kgqn/dot_general | solution.py:28
  23.7 1.8 fusion.10
  25.5 4.0 %fusion.2 = (f32[4,512]{1,0:T(4,128)S(1)}, f32[2048,512,4]{1,0,2:T(8,128)S(1)}) fusion(pred[512,2048]{0,1:T(8,128)(4,1)S(1)} %fusion.20, bf16[512,4,128]{0,2,1:T(8,128)(2,1)S(1)} %bitcast.219, bf16[2048,128]{1,0:T(8,128)(2,1)S(1)} %copy-done), kind=kOutput, calls=%fused_computation.7 | convolution fusion | flops 1086322688 | bytes 18882560 | tf_op jit(solution)/shard_map/qkgd,nkd->kgqn/dot_general | solution.py:28
  29.5 2.5 divide_convert_fusion.2
  32.0 6.4 %fusion.3 = f32[4,512]{1,0:T(4,128)S(1)} fusion(f32[1536,512,4]{1,0,2:T(8,128)} %get-tuple-element.16, f32[4,512]{1,0:T(4,128)S(1)} %get-tuple-element.15, pred[512,1536]{0,1:T(8,128)(4,1)S(1)} %compare_and_fusion), kind=kLoop, calls=%fused_computation.10 | loop fusion | flops 12580864 | bytes 13385728 | tf_op jit(solution)/shard_map/reduce_sum | solution.py:37
  38.4 8.1 %divide_convert_fusion.1 = bf16[512,1,4,128]{0,3,2,1:T(8,128)(2,1)S(1)} fusion(f32[1536,512,4]{1,0,2:T(8,128)} %get-tuple-element.16, f32[4,512]{1,0:T(4,128)S(1)} %get-tuple-element.15, pred[512,1536]{0,1:T(8,128)(4,1)S(1)} %compare_and_fusion, f32[512,4]{0,1:T(4,128)S(1)} %bitcast.228, bf16[2048,128]{1,0:T(8,128)(2,1)S(1)} %copy-done.3), kind=kOutput, calls=%fused_computation.45 | convolution fusion | flops 818413568 | bytes 14303232 | tf_op jit(solution)/shard_map/kgqn,nkd->qkgd/dot_general | solution.py:38
  46.5 3.7 %fusion = f32[4,512]{1,0:T(4,128)S(1)} fusion(f32[2048,512,4]{1,0,2:T(8,128)S(1)} %get-tuple-element.14, f32[4,512]{1,0:T(4,128)S(1)} %get-tuple-element.13, pred[512,2048]{0,1:T(8,128)(4,1)S(1)} %fusion.20), kind=kLoop, calls=%fused_computation.5 | loop fusion | flops 16775168 | bytes 17842176 | tf_op jit(solution)/shard_map/reduce_sum | solution.py:37
  50.2 4.2 %divide_convert_fusion = bf16[512,1,4,128]{0,3,2,1:T(8,128)(2,1)S(1)} fusion(f32[2048,512,4]{1,0,2:T(8,128)S(1)} %get-tuple-element.14, f32[4,512]{1,0:T(4,128)S(1)} %get-tuple-element.13, pred[512,2048]{0,1:T(8,128)(4,1)S(1)} %fusion.20, bf16[2048,128]{1,0:T(8,128)(2,1)S(1)} %copy-done.4, f32[512,4]{0,1:T(4,128)S(1)} %bitcast.226), kind=kOutput, calls=%fused_computation.44 | convolution fusion | flops 1091043328 | bytes 18890752 | tf_op jit(solution)/shard_map/kgqn,nkd->qkgd/dot_general | solution.py:38
  54.7 2.5 copy.87
  57.4 1.9 concatenate.7
  59.8 2.8 gather_fusion
  62.6 8.9 %all-to-all-start = ((bf16[32,1,128,512]{3,2,1,0:T(8,128)(2,1)}), bf16[32,1,128,512]{3,2,1,0:T(8,128)(2,1)}, u32[]{:S(2)}, u32[]{:S(2)}) async-start(bf16[32,1,128,512]{3,2,1,0:T(8,128)(2,1)} %bitcast.214), calls=%async_computation | async-start | bytes 8388608 | tf_op jit(solution)/shard_map/all_to_all | solution.py:102
  71.9 49.1 %all-to-all-done = bf16[32,1,128,512]{3,2,1,0:T(8,128)(2,1)} async-done(((bf16[32,1,128,512]{3,2,1,0:T(8,128)(2,1)}), bf16[32,1,128,512]{3,2,1,0:T(8,128)(2,1)}, u32[]{:S(2)}, u32[]{:S(2)}) %all-to-all-start) | async-done | bytes 4194336 | tf_op jit(solution)/shard_map/all_to_all | solution.py:102
  121.0 2.8 gather_fusion.1
  123.9 15.3 %convolution_convert_fusion = bf16[1024,8192]{1,0:T(8,128)(2,1)} fusion(bf16[1024,512]{1,0:T(8,128)(2,1)S(1)} %bitcast.218, bf16[512,8192]{1,0:T(8,128)(2,1)} %all-gather.2.cloned.1.call-done), kind=kOutput, calls=%fused_computation.4 | convolution fusion | flops 8598323200 | bytes 26214400 | tf_op jit(solution)/shard_map/dot_general | solution.py:110
  139.2 175.5 %reduce-scatter.2.cloned.1.call-done = bf16[128,8192]{1,0:T(8,128)(2,1)} async-done(((bf16[1024,8192]{1,0:T(8,128)(2,1)}), bf16[128,8192]{1,0:T(8,128)(2,1)}) %reduce-scatter.2.cloned.1.call-update) | async-done | bytes 2097168 | tf_op jit(solution)/shard_map/reduce_scatter | solution.py:115
  (47 shorter events, 3.3 us)
Async XLA Ops:
  6.5 3.3 %copy-start.1 = (s32[2048]{0:T(1024)S(1)}, s32[2048]{0:T(1024)}, u32[]{:S(2)}) copy-start(s32[2048]{0:T(1024)} %param.10) | copy-start | bytes 24580
  6.5 3.6 %slice-start = ((s32[2048]{0:T(1024)}), s32[1024]{0:T(1024)S(1)}, s32[]{:S(2)}) async-start(s32[2048]{0:T(1024)} %param.10), calls=%async_computation.4 | async-start | bytes 8192 | tf_op jit(solution)/shard_map/slice | solution.py:63
  6.5 4.5 %copy-start = (bf16[2048,128]{1,0:T(8,128)(2,1)S(1)}, bf16[2048,128]{1,0:T(8,128)(2,1)}, u32[]{:S(2)}) copy-start(bf16[2048,128]{1,0:T(8,128)(2,1)} %param.7) | copy-start | bytes 1572868
  6.5 117.3 %all-gather.2.cloned.1.call-start = ((), (), s32[]{:S(2)}) async-start(), calls=%async_computation.2 | async-start | bytes 8650752 | tf_op jit(solution)/shard_map/all_gather | solution.py:112
  9.8 3.0 copy-start.3
  46.5 3.7 %copy-start.4 = (bf16[2048,128]{1,0:T(8,128)(2,1)S(1)}, bf16[2048,128]{1,0:T(8,128)(2,1)}, u32[]{:S(2)}) copy-start(bf16[2048,128]{1,0:T(8,128)(2,1)} %param.8) | copy-start | bytes 1572868
  54.4 2.8 copy-start.2
  62.6 58.4 %all-to-all-start = ((bf16[32,1,128,512]{3,2,1,0:T(8,128)(2,1)}), bf16[32,1,128,512]{3,2,1,0:T(8,128)(2,1)}, u32[]{:S(2)}, u32[]{:S(2)}) async-start(bf16[32,1,128,512]{3,2,1,0:T(8,128)(2,1)} %bitcast.214), calls=%async_computation | async-start | bytes 8388608 | tf_op jit(solution)/shard_map/all_to_all | solution.py:102
  71.5 243.2 %reduce-scatter.2.cloned.1.call-start = ((), (), s32[]{:S(2)}) async-start(), calls=%async_computation.3 | async-start | bytes 18874368 | tf_op jit(solution)/shard_map/reduce_scatter | solution.py:115
Sparse Core Ops, SparseCore 0:
  9.8 74.5 all-gather.1
  139.3 175.3 reduce-scatter.1
where the time goes:
time: 322 us
  waiting for transfers between devices  225 us (70%)
  matrix products  43.6 us (14%)
  other arithmetic  17.1 us (5%)
  between operations  13.7 us (4%)
  local copies, waits for them, and re-layouts  12.8 us (4%)
  starting transfers between devices  8.93 us (3%)
    reduce_scatter x1, waiting for transfers between devices, on_device(): lax.psum_scatter(partial_sums.astype(jnp.bfloat16), 'mp', scatter_dimensi...  176 us
    all_to_all x1, waiting for transfers between devices, on_device(): lax.all_to_all(outgoing, 'dp', split_axis=0, concat_axis=0, tiled=True)  49.1 us
    dot_general x4, matrix products, attend_block(): jnp.einsum('kgqn,nkd->qkgd', weights.astype(jnp.bfloat16), head_values, p...  16.1 us
    dot_general x1, matrix products, on_device(): jnp.dot(placed, lax.all_gather(out_weight, 'dp', axis=1, tiled=True), pre...  15.3 us
    reduce_sum x4, other arithmetic, attend_block(): row_total = jnp.sum(weights, axis=-1)  12.8 us
    dot_general x4, matrix products, attend_block(): jnp.einsum('qkgd,nkd->kgqn', head_queries, head_keys, preferred_element_t...  12.2 us
    all_to_all x1, starting transfers between devices, on_device(): lax.all_to_all(outgoing, 'dp', split_axis=0, concat_axis=0, tiled=True)  8.89 us
  transfers between devices with their start and end apart: 3, of which 2 were waited for; matrix products, arithmetic and copies ran while one was open for 18% of the time, Pallas kernels for 0%

commit v1 on v0

v1 whole, which is shorter than its diff:
```python
import functools
import math

import jax
import jax.numpy as jnp
from jax import lax
from jax.experimental import pallas as pl
from jax.experimental.pallas import tpu as pltpu
from jax.sharding import Mesh
from jax.sharding import PartitionSpec as P

HEAD = 128
TQ = 256
BLOCK = 128
BAL = 8
PIECE = 4
PLANE = ("y", "x", "c")
MB = 1024 * 1024

def attention_kernel(seg_s, q_ref, k_ref, v_ref, seg_ref, o_ref, s_scr, m_scr):
    heads = q_ref.shape[1] // HEAD
    t = pl.program_id(0)
    q0 = t * TQ
    first_seg = seg_s[q0]
    c = math.log2(math.e) / math.sqrt(HEAD)

    @pl.when(first_seg >= 0)
    def _():
        lo = jnp.int32(0)
        for j in range(pl.num_programs(0) - 1):
            lo += jnp.where((j < t) & (seg_s[j * TQ + TQ - 1] < first_seg), 1, 0).astype(jnp.int32)
        seg_q = jnp.concatenate(
            [
                jnp.transpose(jnp.broadcast_to(seg_ref[:, pl.ds(pl.multiple_of(q0 + r, 128), 128)], (128, 128)))
                for r in range(0, TQ, 128)
            ],
            axis=0,
        )
        seg_q = jnp.concatenate([seg_q] * (TQ // 128), axis=1)

        def scores(j, diagonal):
            k0 = pl.multiple_of(j * TQ, TQ)
            keys = k_ref[pl.ds(k0, TQ), :]
            allowed = seg_q == jnp.broadcast_to(seg_ref[:, pl.ds(k0, TQ)], (TQ, TQ))
            if diagonal:
                allowed &= lax.broadcasted_iota(jnp.int32, (TQ, TQ), 1) <= lax.broadcasted_iota(jnp.int32, (TQ, TQ), 0)
            bias = jnp.where(allowed, 0.0, -1e30).astype(jnp.float32)
            for h in range(heads):
                s = lax.dot_general(
                    q_ref[:, h * HEAD : (h + 1) * HEAD], keys, (((1,), (1,)), ((), ())), preferred_element_type=jnp.float32
                )
                s = s + bias
                s_scr[h, j - lo] = s
                part = jnp.maximum(s[:, :HEAD], s[:, HEAD:])
                if diagonal:
                    m_scr[h] = part
                else:
                    m_scr[h] = jnp.maximum(m_scr[h], part)

        scores(t, True)

        @pl.loop(lo, t)
        def _(j):
            scores(j, False)

        for h in range(heads):
            top = jnp.max(m_scr[h], axis=1, keepdims=True) * c

            def step(j, carry):
                total, acc = carry
                w = jnp.exp2(s_scr[h, j - lo] * c - top)
                total = total + (w[:, :HEAD] + w[:, HEAD:])
                acc = acc + jnp.dot(
                    w.astype(jnp.bfloat16), v_ref[pl.ds(pl.multiple_of(j * TQ, TQ), TQ), :], preferred_element_type=jnp.float32
                )
                return total, acc

            zero = jnp.zeros((TQ, HEAD), jnp.float32)
            total, acc = lax.fori_loop(lo, t + 1, step, (zero, zero))
            o_ref[:, h * HEAD : (h + 1) * HEAD] = (acc / jnp.sum(total, axis=1, keepdims=True)).astype(jnp.bfloat16)


def attention(queries, keys, values, segments):
    rows, cols = queries.shape
    heads = cols // HEAD
    return pl.pallas_call(
        attention_kernel,
        out_shape=jax.ShapeDtypeStruct((rows, cols), jnp.bfloat16),
        grid_spec=pltpu.PrefetchScalarGridSpec(
            num_scalar_prefetch=1,
            grid=(rows // TQ,),
            in_specs=[
                pl.BlockSpec((TQ, cols), lambda t, *_: (t, 0)),
                pl.BlockSpec((rows, HEAD), lambda t, *_: (0, 0)),
                pl.BlockSpec((rows, HEAD), lambda t, *_: (0, 0)),
                pl.BlockSpec((1, rows), lambda t, *_: (0, 0)),
            ],
            out_specs=pl.BlockSpec((TQ, cols), lambda t, *_: (t, 0)),
            scratch_shapes=[
                pltpu.VMEM((heads, 1024 // TQ + 1, TQ, TQ), jnp.float32),
                pltpu.VMEM((heads, TQ, HEAD), jnp.float32),
            ],
        ),
        compiler_params=pltpu.CompilerParams(vmem_limit_bytes=40 * MB),
        cost_estimate=pl.CostEstimate(flops=4 * rows * 1024 * cols, bytes_accessed=6 * MB, transcendentals=rows * 640 * heads),
        name="attention",
    )(segments, queries, keys, values, segments.reshape(1, rows))


def project_kernel(n_parts, order_s, *refs):
    parts, w_ref, o_ref, rows_scr, acc = refs[:n_parts], refs[n_parts], refs[n_parts + 1], refs[n_parts + 2], refs[n_parts + 3]
    step = pl.program_id(0)
    steps = pl.num_programs(0)
    own, near, far, half_a, half_b = parts[0:2], parts[2:4], parts[4:6], parts[6:8], parts[8:10]
    for c in range(2):
        for k, part in enumerate((own[c], near[c], far[c])):
            rows_scr[(k * 2 + c) * BLOCK : (k * 2 + c + 1) * BLOCK, :] = part[0]

        @pl.when(step < steps // 2)
        def _():
            rows_scr[(6 + c) * BLOCK : (7 + c) * BLOCK, :] = half_a[c][0]

        @pl.when(step >= steps // 2)
        def _():
            rows_scr[(6 + c) * BLOCK : (7 + c) * BLOCK, :] = half_b[c][0]

    wide = w_ref.shape[3]
    for x in range(w_ref.shape[0]):
        product = jnp.dot(rows_scr[...], w_ref[x, 0], preferred_element_type=jnp.float32)

        @pl.when(step == 0)
        def _():
            acc[:, x * wide : (x + 1) * wide] = product

        @pl.when(step > 0)
        def _():
            acc[:, x * wide : (x + 1) * wide] += product

    @pl.when(step == steps - 1)
    def _():
        top = lax.broadcasted_iota(jnp.int32, (8, acc.shape[1]), 0) < PIECE

        @pl.loop(0, BLOCK // 8)
        def _(d2):
            low, high = [], []
            for pair in range(4):
                at = [pl.multiple_of(order_s[2 * pair + i] * BLOCK + d2 * 8, 8) for i in range(2)]
                even, odd = acc[pl.ds(at[0], 8), :], acc[pl.ds(at[1], 8), :]
                low.append(jnp.where(top, even, pltpu.roll(odd, PIECE, 0)))
                high.append(jnp.where(top, pltpu.roll(even, PIECE, 0), odd))
            o_ref[2 * d2] = jnp.concatenate(low, axis=0).astype(jnp.bfloat16)
            o_ref[2 * d2 + 1] = jnp.concatenate(high, axis=0).astype(jnp.bfloat16)


def project(order, parts, weights):
    sets, rows, depth = parts[0].shape
    n_x, _, _, wide = weights.shape
    half = sets // 2
    specs = [pl.BlockSpec((1, rows, depth), lambda i, *_: (i, 0, 0))] * 6
    specs += [pl.BlockSpec((1, rows, depth), lambda i, *_: (jnp.minimum(i, half - 1), 0, 0))] * 2
    specs += [pl.BlockSpec((1, rows, depth), lambda i, *_: (jnp.maximum(i - half, 0), 0, 0))] * 2
    specs += [pl.BlockSpec((n_x, 1, depth, wide), lambda i, *_: (0, i, 0, 0))]
    groups = rows // PIECE
    return pl.pallas_call(
        functools.partial(project_kernel, len(parts)),
        out_shape=jax.ShapeDtypeStruct((groups, 8 * PIECE, n_x * wide), jnp.bfloat16),
        grid_spec=pltpu.PrefetchScalarGridSpec(
            num_scalar_prefetch=1,
            grid=(sets,),
            in_specs=specs,
            out_specs=pl.BlockSpec((groups, 8 * PIECE, n_x * wide), lambda i, *_: (0, 0, 0)),
            scratch_shapes=[
                pltpu.VMEM((8 * rows, depth), jnp.bfloat16),
                pltpu.VMEM((8 * rows, n_x * wide), jnp.float32),
            ],
        ),
        compiler_params=pltpu.CompilerParams(vmem_limit_bytes=40 * MB),
        cost_estimate=pl.CostEstimate(flops=16 * rows * sets * depth * n_x * wide, bytes_accessed=18 * MB, transcendentals=0),
        name="project",
    )(order, *parts, weights)


def gather_rows_of_slots(mine):
    n_y, half = lax.axis_size("y"), mine.shape[0] // 2
    up = [(i, (i + 1) % n_y) for i in range(n_y)]
    down = [(i, (i - 1) % n_y) for i in range(n_y)]
    other = [(0, 1), (1, 0)]
    from_below = lax.ppermute(mine, "y", up)
    from_above = lax.ppermute(mine, "y", down)
    far_a = lax.ppermute(from_below[:half], "y", up)
    far_b = lax.ppermute(from_above[half:], "y", down)
    parts = []
    for part in (mine, from_below, from_above, far_a, far_b):
        parts += [part, lax.ppermute(part, "c", other)]
    return parts


def on_device(queries, keys, values, out_weight, segments, send_plan):
    n_y, n_x, n_c, n_z = (lax.axis_size(a) for a in ("y", "x", "c", "z"))
    groups = n_y * n_x * n_c
    rows, cols = queries.shape
    blocks = rows // BLOCK
    weights = lax.all_gather(out_weight, ("x", "z")).reshape(n_x, n_z, *out_weight.shape)
    attended = attention(queries, keys, values, segments)
    pieces = attended.reshape(blocks, n_x, n_y, n_c, PIECE, cols).transpose(2, 1, 3, 0, 4, 5)
    arrived = lax.all_to_all(pieces.reshape(groups, blocks * PIECE, cols), PLANE, 0, 0, tiled=True)
    slots = jnp.arange(groups * BAL)
    block_of = jnp.sum(
        jnp.where(send_plan[None, :] == slots[:, None], jnp.arange(groups * blocks)[None, :], 0), axis=1, dtype=jnp.int32
    )
    block_of = block_of.reshape(groups, BAL).T.reshape(-1)
    row_of = (block_of[:, None] * PIECE + jnp.arange(PIECE)[None, :]).reshape(-1)
    live = jnp.take(arrived.reshape(groups * blocks * PIECE, cols), row_of, axis=0, mode="clip")
    mine = lax.all_to_all(live.reshape(n_z, groups * PIECE, cols), "z", 0, 0, tiled=True)
    parts = gather_rows_of_slots(mine)
    my_y, my_c = lax.axis_index("y"), lax.axis_index("c")
    place = jnp.array([0, 2, 6, 4], jnp.int32)
    wanted = jnp.arange(n_y * n_c)
    order = place[(my_y - wanted // n_c) % n_y] + (my_c != wanted % n_c)
    projected = project(order.astype(jnp.int32), parts, weights)
    home = lax.all_to_all(projected, PLANE, 0, 0, tiled=True)
    home = home.reshape(n_y, n_x, n_c, n_y * n_c * PIECE, n_x, -1).transpose(1, 3, 0, 4, 2, 5)
    return home.reshape(BLOCK, -1)


def solution(mesh):
    fine = Mesh(mesh.devices.reshape(4, 4, 2, 8), ("y", "x", "c", "z"))
    in_specs = (P(PLANE, "z"), P(PLANE, "z"), P(PLANE, "z"), P("z", PLANE), P(PLANE), P())
    return jax.shard_map(on_device, mesh=fine, in_specs=in_specs, out_specs=P((*PLANE, "z"), None), check_vma=False)
```

time: 322 us -> 273 us (0.85)
  waiting for transfers between devices: 225 us -> 61.9 us
  blocking collectives: 0 us -> 88.3 us
  matrix products: 43.6 us -> 0 us
  starting transfers between devices: 8.93 us -> 51.3 us
  Pallas kernels: 0 us -> 32.9 us
  other arithmetic: 17.1 us -> 0.3 us
  local copies, waits for them, and re-layouts: 12.8 us -> 26.5 us
    reduce_scatter x1 -> x0, waiting for transfers between devices: 176 us -> none  [on_device(): lax.psum_scatter(partial_sums.astype(jnp.bfloat16), 'mp', scatter_dimensi...]
    all_to_all x0 -> x2, blocking collectives: none -> 88.3 us  [the longest x1 48.2 us: on_device(): lax.all_to_all(live.reshape(n_z, groups * PIECE, cols), 'z', 0, 0, tiled=...]
    dot_general x9 -> x0, matrix products: 43.6 us -> none  [the longest x4 16.1 us: attend_block(): jnp.einsum('kgqn,nkd->qkgd', weights.astype(jnp.bfloat16), head_values, p...]
    pallas_call x0 -> x2, Pallas kernels: none -> 32.9 us  [the longest x1 30.3 us: project(): pl.pallas_call(functools.partial(project_kernel, len(parts)), out_shape=j...]
    all_to_all x1, starting transfers between devices: 8.89 us -> 33.2 us  [on_device(): lax.all_to_all(pieces.reshape(groups, blocks * PIECE, cols), PLANE, 0, 0,...]
    ppermute x0 -> x9, waiting for transfers between devices: none -> 23.2 us  [the longest x1 16.5 us: gather_rows_of_slots(): from_above = lax.ppermute(mine, 'y', down)]
    ppermute x0 -> x9, starting transfers between devices: none -> 18.2 us  [the longest x5 13.2 us: gather_rows_of_slots(): parts += [part, lax.ppermute(part, 'c', other)]]
    reduce_sum x7 -> x1, other arithmetic: 13.2 us -> 0.14 us  [on_device(): jnp.sum(jnp.where(send_plan[None, :] == slots[:, None], jnp.arange(groups...]
  transfers between devices with their start and end apart: 3 -> 11, of which waited for: 2 -> 4; matrix products, arithmetic and copies ran while one was open for 18% -> 4% of each run, Pallas kernels for 0% -> 1%
where the time goes in v1:
time: 273 us; the launch traced here: 275 us
  blocking collectives  88.3 us (32%)
  waiting for transfers between devices  61.9 us (23%)
  starting transfers between devices  51.3 us (19%)
  Pallas kernels  32.9 us (12%)
  local copies, waits for them, and re-layouts  26.5 us (10%)
  between operations  13.5 us (5%)
    all_to_all x1, blocking collectives, on_device(): lax.all_to_all(live.reshape(n_z, groups * PIECE, cols), 'z', 0, 0, tiled=...  48.2 us
    all_to_all x1, blocking collectives, on_device(): home = lax.all_to_all(projected, PLANE, 0, 0, tiled=True)  40.1 us
    all_to_all x1, waiting for transfers between devices, on_device(): lax.all_to_all(pieces.reshape(groups, blocks * PIECE, cols), PLANE, 0, 0,...  38 us
    all_to_all x1, starting transfers between devices, on_device(): lax.all_to_all(pieces.reshape(groups, blocks * PIECE, cols), PLANE, 0, 0,...  33.2 us
    pallas_call x1, Pallas kernels, project(): pl.pallas_call(functools.partial(project_kernel, len(parts)), out_shape=j...  30.3 us
    ppermute x1, waiting for transfers between devices, gather_rows_of_slots(): from_above = lax.ppermute(mine, 'y', down)  16.5 us
    ppermute x5, starting transfers between devices, gather_rows_of_slots(): parts += [part, lax.ppermute(part, 'c', other)]  13.2 us
    ppermute x1, waiting for transfers between devices, gather_rows_of_slots(): far_b = lax.ppermute(from_above[half:], 'y', down)  5.53 us
  transfers between devices with their start and end apart: 11, of which 4 were waited for; matrix products, arithmetic and copies ran while one was open for 4% of the time, Pallas kernels for 1%

profile of v1, /device:TPU:1, one launch (start us, length us, event | category | flops | bytes accessed | tf_op | source)
XLA Modules:
  0.0 274.9 jit_solution(12469216586527076522)
XLA Ops:
  7.3 1.6 copy-done
  8.9 1.0 copy-done.1
  11.6 2.7 attention.1
  14.3 2.0 reshape.141
  16.3 2.7 copy.16
  19.0 2.0 reshape.142
  21.0 33.2 %all-to-all-start = ((bf16[32,64,512]{2,1,0:T(8,128)(2,1)}), bf16[32,64,512]{2,1,0:T(8,128)(2,1)S(1)}, u32[]{:S(2)}, u32[]{:S(2)}) async-start(bf16[32,64,512]{2,1,0:T(8,128)(2,1)} %reshape.142), calls=%async_computation | async-start | bytes 4194304 | tf_op jit(solution)/shard_map/all_to_all | solution.py:206
  54.9 38.0 %all-to-all-done = bf16[32,64,512]{2,1,0:T(8,128)(2,1)S(1)} async-done(((bf16[32,64,512]{2,1,0:T(8,128)(2,1)}), bf16[32,64,512]{2,1,0:T(8,128)(2,1)S(1)}, u32[]{:S(2)}, u32[]{:S(2)}) %all-to-all-start) | async-done | bytes 2097184 | tf_op jit(solution)/shard_map/all_to_all | solution.py:206
  92.9 4.0 %gather_fusion.1 = bf16[1024,512]{1,0:T(8,128)(2,1)S(1)} fusion(bf16[2048,512]{1,0:T(8,128)(2,1)S(1)} %bitcast.12, s32[1024]{0:T(1024)S(1)} %broadcast_clamp_fusion), kind=kCustom, calls=%fused_computation.1 | custom fusion | bytes 2101248 | tf_op jit(solution)/shard_map/jit(_take)/gather | solution.py:213
  96.9 48.2 %all_to_all.15.refs_0_ = bf16[8,128,512]{2,1,0:T(8,128)(2,1)S(1)} all-to-all(bf16[8,128,512]{2,1,0:T(8,128)(2,1)S(1)} %bitcast.15), channel_id=1, replica_groups=mesh['y'=4,'x'=4,'c'=2,'z'=8] {'z'}, dimensions={0} | all-to-all | bytes 2097152 | tf_op jit(solution)/shard_map/all_to_all | solution.py:214
  145.1 1.4 collective-permute-start.3
  147.0 3.6 %collective-permute-start = (bf16[8,128,512]{2,1,0:T(8,128)(2,1)S(1)}, bf16[8,128,512]{2,1,0:T(8,128)(2,1)}, u32[]{:S(2)}, u32[]{:S(2)}) collective-permute-start(bf16[8,128,512]{2,1,0:T(8,128)(2,1)S(1)} %all_to_all.15.refs_0_), channel_id=1, source_target_pairs={{0,8},{8,0},{1,9},{9,1},{2,10},{10,2},{3,11},{11,3},{4,12},{12,4},... | collective-permute-start | bytes 3145736 | tf_op jit(solution)/shard_map/ppermute | solution.py:194
  150.7 16.5 %collective-permute-done.3.refs_4_ = bf16[8,128,512]{2,1,0:T(8,128)(2,1)S(1)} collective-permute-done((bf16[8,128,512]{2,1,0:T(8,128)(2,1)S(1)}, bf16[8,128,512]{2,1,0:T(8,128)(2,1)S(1)}, u32[]{:S(2)}, u32[]{:S(2)}) %collective-permute-start.3) | collective-permute-done | bytes 1048608 | tf_op jit(solution)/shard_map/ppermute | solution.py:189
  167.2 2.4 collective-permute-start.7
  170.2 3.7 %collective-permute-start.4 = (bf16[8,128,512]{2,1,0:T(8,128)(2,1)S(1)}, bf16[8,128,512]{2,1,0:T(8,128)(2,1)}, u32[]{:S(2)}, u32[]{:S(2)}) collective-permute-start(bf16[8,128,512]{2,1,0:T(8,128)(2,1)S(1)} %collective-permute-done.3.refs_4_), channel_id=1, source_target_pairs={{0,8},{8,0},{1,9},{9,1},{2,10},{10,2},{3,11},{11,3},{4,12},{12,4},... | collective-permute-start | bytes 3145736 | tf_op jit(solution)/shard_map/ppermute | solution.py:194
  174.0 5.5 %collective-permute-done.7.refs_8_ = bf16[4,128,512]{2,1,0:T(8,128)(2,1)} collective-permute-done((bf16[4,128,512]{2,1,0:T(8,128)(2,1)S(1)}, bf16[4,128,512]{2,1,0:T(8,128)(2,1)}, u32[]{:S(2)}, u32[]{:S(2)}) %collective-permute-start.7) | collective-permute-done | bytes 524320 | tf_op jit(solution)/shard_map/ppermute | solution.py:191
  179.5 3.6 %collective-permute-start.8 = (bf16[4,128,512]{2,1,0:T(8,128)(2,1)}, bf16[4,128,512]{2,1,0:T(8,128)(2,1)}, u32[]{:S(2)}, u32[]{:S(2)}) collective-permute-start(bf16[4,128,512]{2,1,0:T(8,128)(2,1)} %collective-permute-done.7.refs_8_), channel_id=1, source_target_pairs={{0,8},{8,0},{1,9},{9,1},{2,10},{10,2},{3,11},{11,3},{4,12},{12,4},... | collective-permute-start | bytes 1572872 | tf_op jit(solution)/shard_map/ppermute | solution.py:194
  183.1 2.2 collective-permute-start.6
  186.0 1.2 collective-permute-done.6.refs_7_
  187.2 30.3 %project.1 = bf16[32,32,1024]{2,1,0:T(8,128)(2,1)S(1)} custom-call(s32[8]{0:T(128)S(1)} %fusion.1.order_s, bf16[8,128,512]{2,1,0:T(8,128)(2,1)S(1)} %all_to_all.15.refs_0_, bf16[8,128,512]{2,1,0:T(8,128)(2,1)} %collective-permute-done.refs_1_, bf16[8,128,512]{2,1,0:T(8,128)(2,1)S(1)} %collective-permute-done.1.refs_2_, ...), custom_call_target="tpu_custom_call" | custom-call | flops 8589934592 | bytes 18874368 | tf_op jit(solution)/shard_map/project/pallas_call | solution.py:164
  217.5 40.1 %all_to_all.16 = bf16[32,32,1024]{2,1,0:T(8,128)(2,1)S(1)} all-to-all(bf16[32,32,1024]{2,1,0:T(8,128)(2,1)S(1)} %project.1), channel_id=1, replica_groups=mesh['y'=4,'x'=4,'c'=2,'z'=8] {'y','x','c'}, dimensions={0} | all-to-all | bytes 4194304 | tf_op jit(solution)/shard_map/all_to_all | solution.py:221
  257.7 2.7 reshape.146
  260.4 4.8 %copy.14 = bf16[4,32,4,4,2,256]{5,4,3,2,1,0:T(2,128)(2,1)S(1)} copy(bf16[4,32,4,4,2,256]{5,3,1,4,0,2:T(4,128)(2,1)} %bitcast.14) | data formatting | bytes 4194304 | tf_op jit(solution)/shard_map/transpose | solution.py:222
  265.2 2.8 %reshape.147 = bf16[128,8192]{1,0:T(8,128)(2,1)} reshape(bf16[4,32,4,4,2,256]{5,4,3,2,1,0:T(2,128)(2,1)S(1)} %copy.14) | data formatting | bytes 4194304 | tf_op jit(solution)/shard_map/reshape | solution.py:223
  (36 shorter events, 5.1 us)
Async XLA Ops:
  6.5 180.7 %all-gather.3.cloned.1.call-start = ((), (), s32[]{:S(2)}) async-start(), calls=%async_computation.3 | async-start | bytes 8650752 | tf_op jit(solution)/shard_map/all_gather | solution.py:203
  7.3 1.6 copy-start
  8.8 1.0 copy-start.1
  9.9 1.0 copy-start.2
  10.9 0.7 copy-start.3
  21.0 33.2 %copy-start.5 = (s32[512]{0:T(512)S(1)}, s32[512]{0:T(512)}, u32[]{:S(2)}) copy-start(s32[512]{0:T(512)} %param.12) | copy-start | bytes 6148
  21.0 71.9 %all-to-all-start = ((bf16[32,64,512]{2,1,0:T(8,128)(2,1)}), bf16[32,64,512]{2,1,0:T(8,128)(2,1)S(1)}, u32[]{:S(2)}, u32[]{:S(2)}) async-start(bf16[32,64,512]{2,1,0:T(8,128)(2,1)} %reshape.142), calls=%async_computation | async-start | bytes 4194304 | tf_op jit(solution)/shard_map/all_to_all | solution.py:206
  96.9 88.5 %copy-start.4 = (s32[4]{0:T(128)S(1)}, s32[4]{0:T(128)}, u32[]{:S(2)}) copy-start(s32[4]{0:T(128)} %constant.57.clone) | copy-start | bytes 52
  145.1 22.1 %collective-permute-start.3 = (bf16[8,128,512]{2,1,0:T(8,128)(2,1)S(1)}, bf16[8,128,512]{2,1,0:T(8,128)(2,1)S(1)}, u32[]{:S(2)}, u32[]{:S(2)}) collective-permute-start(bf16[8,128,512]{2,1,0:T(8,128)(2,1)S(1)} %all_to_all.15.refs_0_), channel_id=1, source_target_pairs={{0,192},{64,0},{128,64},{192,128},{1,193},{65,1},{129,65},{193,129... | collective-permute-start | bytes 3145736 | tf_op jit(solution)/shard_map/ppermute | solution.py:189
  146.5 23.1 %collective-permute-start.1 = (bf16[8,128,512]{2,1,0:T(8,128)(2,1)S(1)}, bf16[8,128,512]{2,1,0:T(8,128)(2,1)S(1)}, u32[]{:S(2)}, u32[]{:S(2)}) collective-permute-start(bf16[8,128,512]{2,1,0:T(8,128)(2,1)S(1)} %all_to_all.15.refs_0_), channel_id=1, source_target_pairs={{0,64},{64,128},{128,192},{192,0},{1,65},{65,129},{129,193},{193,1... | collective-permute-start | bytes 3145736 | tf_op jit(solution)/shard_map/ppermute | solution.py:188
  147.0 39.0 %collective-permute-start = (bf16[8,128,512]{2,1,0:T(8,128)(2,1)S(1)}, bf16[8,128,512]{2,1,0:T(8,128)(2,1)}, u32[]{:S(2)}, u32[]{:S(2)}) collective-permute-start(bf16[8,128,512]{2,1,0:T(8,128)(2,1)S(1)} %all_to_all.15.refs_0_), channel_id=1, source_target_pairs={{0,8},{8,0},{1,9},{9,1},{2,10},{10,2},{3,11},{11,3},{4,12},{12,4},... | collective-permute-start | bytes 3145736 | tf_op jit(solution)/shard_map/ppermute | solution.py:194
  167.2 12.3 %collective-permute-start.7 = (bf16[4,128,512]{2,1,0:T(8,128)(2,1)S(1)}, bf16[4,128,512]{2,1,0:T(8,128)(2,1)}, u32[]{:S(2)}, u32[]{:S(2)}) collective-permute-start(bf16[4,128,512]{2,1,0:T(8,128)(2,1)S(1)} %slice.13), channel_id=1, source_target_pairs={{0,192},{64,0},{128,64},{192,128},{1,193},{65,1},{129,65},{193,129... | collective-permute-start | bytes 1572872 | tf_op jit(solution)/shard_map/ppermute | solution.py:191
  169.6 13.5 %collective-permute-start.5 = (bf16[4,128,512]{2,1,0:T(8,128)(2,1)S(1)}, bf16[4,128,512]{2,1,0:T(8,128)(2,1)}, u32[]{:S(2)}, u32[]{:S(2)}) collective-permute-start(bf16[4,128,512]{2,1,0:T(8,128)(2,1)S(1)} %slice.12), channel_id=1, source_target_pairs={{0,64},{64,128},{128,192},{192,0},{1,65},{65,129},{129,193},{193,1... | collective-permute-start | bytes 1572872 | tf_op jit(solution)/shard_map/ppermute | solution.py:190
  170.2 17.0 %collective-permute-start.4 = (bf16[8,128,512]{2,1,0:T(8,128)(2,1)S(1)}, bf16[8,128,512]{2,1,0:T(8,128)(2,1)}, u32[]{:S(2)}, u32[]{:S(2)}) collective-permute-start(bf16[8,128,512]{2,1,0:T(8,128)(2,1)S(1)} %collective-permute-done.3.refs_4_), channel_id=1, source_target_pairs={{0,8},{8,0},{1,9},{9,1},{2,10},{10,2},{3,11},{11,3},{4,12},{12,4},... | collective-permute-start | bytes 3145736 | tf_op jit(solution)/shard_map/ppermute | solution.py:194
  173.9 13.3 %collective-permute-start.2 = (bf16[8,128,512]{2,1,0:T(8,128)(2,1)S(1)}, bf16[8,128,512]{2,1,0:T(8,128)(2,1)}, u32[]{:S(2)}, u32[]{:S(2)}) collective-permute-start(bf16[8,128,512]{2,1,0:T(8,128)(2,1)S(1)} %collective-permute-done.1.refs_2_), channel_id=1, source_target_pairs={{0,8},{8,0},{1,9},{9,1},{2,10},{10,2},{3,11},{11,3},{4,12},{12,4},... | collective-permute-start | bytes 3145736 | tf_op jit(solution)/shard_map/ppermute | solution.py:194
  179.5 6.5 %collective-permute-start.8 = (bf16[4,128,512]{2,1,0:T(8,128)(2,1)}, bf16[4,128,512]{2,1,0:T(8,128)(2,1)}, u32[]{:S(2)}, u32[]{:S(2)}) collective-permute-start(bf16[4,128,512]{2,1,0:T(8,128)(2,1)} %collective-permute-done.7.refs_8_), channel_id=1, source_target_pairs={{0,8},{8,0},{1,9},{9,1},{2,10},{10,2},{3,11},{11,3},{4,12},{12,4},... | collective-permute-start | bytes 1572872 | tf_op jit(solution)/shard_map/ppermute | solution.py:194
  183.1 4.1 %collective-permute-start.6 = (bf16[4,128,512]{2,1,0:T(8,128)(2,1)}, bf16[4,128,512]{2,1,0:T(8,128)(2,1)}, u32[]{:S(2)}, u32[]{:S(2)}) collective-permute-start(bf16[4,128,512]{2,1,0:T(8,128)(2,1)} %collective-permute-done.5.refs_6_), channel_id=1, source_target_pairs={{0,8},{8,0},{1,9},{9,1},{2,10},{10,2},{3,11},{11,3},{4,12},{12,4},... | collective-permute-start | bytes 1572872 | tf_op jit(solution)/shard_map/ppermute | solution.py:194
Sparse Core Ops, SparseCore 0:
  9.9 140.2 all-gather.2

commit v2 on v1

v2 whole, which is shorter than its diff:
```python
import functools
import math

import jax
import jax.numpy as jnp
from jax import lax
from jax.experimental import pallas as pl
from jax.experimental.pallas import tpu as pltpu
from jax.sharding import Mesh
from jax.sharding import PartitionSpec as P

HEAD = 128
TQ = 512
LONGEST = 1024
BLOCK = 128
BAL = 8
PIECE = 4
PLANE = ("y", "x", "c")
MB = 1024 * 1024


def swap_halves(even, odd, axis):
    top = lax.broadcasted_iota(jnp.int32, even.shape, axis) < PIECE
    return jnp.where(top, even, pltpu.roll(odd, PIECE, axis)), jnp.where(top, pltpu.roll(even, PIECE, axis), odd)


def attention_kernel(seg_s, q_ref, k_ref, v_ref, seg_ref, o_ref, bias_scr):
    heads = q_ref.shape[1] // HEAD
    t = pl.program_id(0)
    q0 = t * TQ
    first = seg_s[q0]
    scale = math.log2(math.e) / math.sqrt(HEAD)

    def attend(n):
        k0 = pl.multiple_of((t + 1 - n) * TQ, TQ)
        keys = k_ref[pl.ds(k0, n * TQ), :]
        values = v_ref[pl.ds(k0, n * TQ), :]
        seg_q = jnp.concatenate(
            [
                jnp.transpose(jnp.broadcast_to(seg_ref[:, pl.ds(pl.multiple_of(q0 + r, 128), 128)], (128, 128)))
                for r in range(0, TQ, 128)
            ],
            axis=0,
        )
        seg_q = jnp.concatenate([seg_q] * (TQ // 128), axis=1)
        for j in range(n):
            seg_k = seg_ref[:, pl.ds(pl.multiple_of(k0 + j * TQ, TQ), TQ)]
            allowed = seg_q == jnp.broadcast_to(seg_k, (TQ, TQ))
            if j == n - 1:
                allowed &= lax.broadcasted_iota(jnp.int32, (TQ, TQ), 1) <= lax.broadcasted_iota(jnp.int32, (TQ, TQ), 0)
            bias_scr[:, j * TQ : (j + 1) * TQ] = jnp.where(allowed, 0.0, -1e30).astype(jnp.float32)
        for h in range(heads):
            cols = slice(h * HEAD, (h + 1) * HEAD)
            scores = lax.dot_general(q_ref[:, cols], keys, (((1,), (1,)), ((), ())), preferred_element_type=jnp.float32)
            scores = scores + bias_scr[:, : n * TQ]
            top = jnp.max(scores, axis=1, keepdims=True) * scale
            weights = jnp.exp2(scores * scale - top)
            total = jnp.sum(weights, axis=1, keepdims=True)
            mixed = jnp.dot(weights.astype(jnp.bfloat16), values, preferred_element_type=jnp.float32) / total
            mixed = mixed.reshape(TQ // BLOCK, BLOCK // 8, 8, HEAD)
            runs = []
            for b in range(0, TQ // BLOCK, 2):
                low, high = swap_halves(mixed[b], mixed[b + 1], 1)
                sides = jnp.stack([low, high], axis=1).reshape(4, 4, 2, 8, HEAD)
                runs.append(sides.swapaxes(0, 1).reshape(BLOCK // PIECE, 8, HEAD))
            o_ref[:, :, cols] = jnp.concatenate(runs, axis=1).astype(jnp.bfloat16)

    @pl.when(first >= 0)
    def _():
        tiles = jnp.int32(1)
        for j in range(pl.num_programs(0) - 1):
            tiles += jnp.where((j < t) & (seg_s[j * TQ + TQ - 1] >= first), 1, 0).astype(jnp.int32)
        for n in range(1, LONGEST // TQ + 2):

            @pl.when(tiles == n)
            def _():
                attend(n)


def attention(queries, keys, values, segments):
    rows, cols = queries.shape
    heads = cols // HEAD
    groups = BLOCK // PIECE
    return pl.pallas_call(
        attention_kernel,
        out_shape=jax.ShapeDtypeStruct((groups, rows // groups, cols), jnp.bfloat16),
        grid_spec=pltpu.PrefetchScalarGridSpec(
            num_scalar_prefetch=1,
            grid=(rows // TQ,),
            in_specs=[
                pl.BlockSpec((TQ, cols), lambda t, *_: (t, 0)),
                pl.BlockSpec((rows, HEAD), lambda t, *_: (0, 0)),
                pl.BlockSpec((rows, HEAD), lambda t, *_: (0, 0)),
                pl.BlockSpec((1, rows), lambda t, *_: (0, 0)),
            ],
            out_specs=pl.BlockSpec((groups, TQ // groups, cols), lambda t, *_: (0, t, 0)),
            scratch_shapes=[pltpu.VMEM((TQ, LONGEST + TQ), jnp.float32)],
        ),
        compiler_params=pltpu.CompilerParams(vmem_limit_bytes=58 * MB),
        cost_estimate=pl.CostEstimate(flops=4 * rows * LONGEST * cols, bytes_accessed=6 * MB, transcendentals=rows * 640 * heads),
        name="attention",
    )(segments, queries, keys, values, segments.reshape(1, rows))


def project_kernel(order_s, *refs):
    parts, weights, o_ref = refs[:8], refs[8:12], refs[12]
    rows_scr, w_scr, product, row_sems, w_sems = refs[13:]
    sets, depth = w_scr.shape[1], w_scr.shape[2]
    step = pl.program_id(0)

    def row_copy(k, z):
        into = rows_scr.at[pl.ds(k * BLOCK, BLOCK), pl.ds(z * depth, depth)]
        return pltpu.make_async_copy(parts[k].at[z], into, row_sems.at[k * sets + z])

    def weight_copy(k):
        return pltpu.make_async_copy(weights[k], w_scr.at[k], w_sems.at[k])

    @pl.when(step == 0)
    def _():
        weight_copy(0).start()
        for z in range(sets):
            for k in range(len(parts)):
                row_copy(k, z).start()
        for k in range(1, len(weights)):
            weight_copy(k).start()
        for z in range(sets):
            for k in range(len(parts)):
                row_copy(k, z).wait()

    for k in range(len(weights)):

        @pl.when(step == k)
        def _():
            weight_copy(k).wait()

    w = w_scr[step].reshape(sets * depth, w_scr.shape[3])
    product[...] = jnp.dot(rows_scr[...], w, preferred_element_type=jnp.float32)
    for d2 in range(BLOCK // 8):
        low, high = [], []
        for pair in range(4):
            at = [pl.multiple_of(order_s[2 * pair + i] * BLOCK + d2 * 8, 8) for i in range(2)]
            both = swap_halves(product[pl.ds(at[0], 8), :], product[pl.ds(at[1], 8), :], 0)
            low.append(both[0])
            high.append(both[1])
        o_ref[2 * d2] = jnp.concatenate(low, axis=0).astype(jnp.bfloat16)
        o_ref[2 * d2 + 1] = jnp.concatenate(high, axis=0).astype(jnp.bfloat16)


def project(order, parts, weights):
    sets, rows, depth = parts[0].shape
    wide = weights[0].shape[2]
    n_x = 4
    groups = rows // PIECE
    return pl.pallas_call(
        project_kernel,
        out_shape=jax.ShapeDtypeStruct((groups, 8 * PIECE, n_x * wide), jnp.bfloat16),
        grid_spec=pltpu.PrefetchScalarGridSpec(
            num_scalar_prefetch=1,
            grid=(n_x,),
            in_specs=[pl.BlockSpec(memory_space=pl.ANY)] * 12,
            out_specs=pl.BlockSpec((groups, 8 * PIECE, wide), lambda k, order_s: (0, 0, order_s[8 + k])),
            scratch_shapes=[
                pltpu.VMEM((8 * rows, sets * depth), jnp.bfloat16),
                pltpu.VMEM((n_x, sets, depth, wide), jnp.bfloat16),
                pltpu.VMEM((8 * rows, wide), jnp.float32),
                pltpu.SemaphoreType.DMA((8 * sets,)),
                pltpu.SemaphoreType.DMA((n_x,)),
            ],
        ),
        compiler_params=pltpu.CompilerParams(vmem_limit_bytes=56 * MB),
        cost_estimate=pl.CostEstimate(flops=16 * rows * sets * depth * n_x * wide, bytes_accessed=18 * MB, transcendentals=0),
        name="project",
    )(order, *parts, *weights)


def arrange_kernel(i_ref, o_ref):
    n_y, _, n_c, rows, cols = i_ref.shape
    n_x = pl.num_programs(0)
    wide = cols // n_x
    for y in range(n_y):
        for x in range(n_x):
            for c in range(n_c):
                at = ((y * n_x + x) * n_c + c) * wide
                o_ref[:, at : at + wide] = i_ref[y, 0, c, :, x * wide : (x + 1) * wide]


def arrange(home):
    n_y, n_x, n_c = 4, 4, 2
    _, rows, cols = home.shape
    return pl.pallas_call(
        arrange_kernel,
        out_shape=jax.ShapeDtypeStruct((n_x * rows, n_y * n_c * cols), jnp.bfloat16),
        grid=(n_x,),
        in_specs=[pl.BlockSpec((n_y, 1, n_c, rows, cols), lambda x: (0, x, 0, 0, 0))],
        out_specs=pl.BlockSpec((rows, n_y * n_c * cols), lambda x: (x, 0)),
        compiler_params=pltpu.CompilerParams(vmem_limit_bytes=56 * MB),
        cost_estimate=pl.CostEstimate(flops=0, bytes_accessed=4 * MB, transcendentals=0),
        name="arrange",
    )(home.reshape(n_y, n_x, n_c, rows, cols))


def neighbours(axis, n, apart):
    return [(i, (i + apart) % n) for i in range(n)]


def hop(mine, turn):
    n_y, n_c = lax.axis_size("y"), lax.axis_size("c")
    pairs = [(y * n_c + c, (y + turn * (1 - 2 * c)) % n_y * n_c + c) for y in range(n_y) for c in range(n_c)]
    return lax.ppermute(mine, ("y", "c"), pairs)


def on_device(queries, keys, values, out_weight, segments, send_plan):
    n_y, n_x, n_c, n_z = (lax.axis_size(a) for a in ("y", "x", "c", "z"))
    groups = n_y * n_x * n_c
    rows, cols = queries.shape
    blocks = rows // BLOCK
    w_across = lax.all_gather(lax.ppermute(out_weight, "x", neighbours("x", n_x, 2)), "z")
    w_own = lax.all_gather(out_weight, "z")
    pieces = attention(queries, keys, values, segments)
    arrived = lax.all_to_all(pieces, PLANE, 0, 0, tiled=True)
    w_own, arrived = lax.optimization_barrier((w_own, arrived))
    w_below, w_above = (lax.ppermute(w_own, "x", neighbours("x", n_x, turn)) for turn in (1, -1))
    slots = jnp.arange(groups * BAL)
    block_of = jnp.sum(
        jnp.where(send_plan[None, :] == slots[:, None], jnp.arange(groups * blocks)[None, :], 0), axis=1, dtype=jnp.int32
    )
    block_of = block_of.reshape(groups, BAL).T.reshape(-1)
    row_of = (block_of[:, None] * PIECE + jnp.arange(PIECE)[None, :]).reshape(-1)
    live = jnp.take(arrived.reshape(groups * blocks * PIECE, cols), row_of, axis=0, mode="clip")
    mine = lax.all_to_all(live.reshape(n_z, groups * PIECE, cols), "z", 0, 0, tiled=True)
    ahead, behind = hop(mine, 1), hop(mine, -1)
    parts = []
    for part in (mine, ahead, behind, hop(ahead, 1)):
        parts += [part, lax.ppermute(part, "c", [(0, 1), (1, 0)])]
    my_y, my_x, my_c = (lax.axis_index(a) for a in PLANE)
    from_y, from_c = jnp.divmod(jnp.arange(n_y * n_c), n_c)
    place = jnp.array([[0, 2, 6, 4], [0, 4, 6, 2]], jnp.int32)
    order = place[from_c, (my_y - from_y) % n_y] + (my_c != from_c)
    order = jnp.concatenate([order, (my_x + jnp.array([0, 3, 1, 2], jnp.int32)) % n_x])
    projected = project(order.astype(jnp.int32), parts, (w_own, w_below, w_above, w_across))
    return arrange(lax.all_to_all(projected, PLANE, 0, 0, tiled=True))


def solution(mesh):
    fine = Mesh(mesh.devices.reshape(4, 4, 2, 8), ("y", "x", "c", "z"))
    in_specs = (P(PLANE, "z"), P(PLANE, "z"), P(PLANE, "z"), P("z", PLANE), P(PLANE), P())
    return jax.shard_map(on_device, mesh=fine, in_specs=in_specs, out_specs=P((*PLANE, "z"), None), check_vma=False)
```

time: 273 us -> 210 us (0.77)
  blocking collectives: 88.3 us -> 33.3 us
  local copies, waits for them, and re-layouts: 26.5 us -> 6.8 us
  waiting for transfers between devices: 61.9 us -> 78.4 us
  starting transfers between devices: 51.3 us -> 44.7 us
    all_to_all x2 -> x1, blocking collectives: 88.3 us -> 33.3 us  [on_device(): return arrange(lax.all_to_all(projected, PLANE, 0, 0, tiled=True))]
    all_to_all x1 -> x2, starting transfers between devices: 33.2 us -> 17.7 us  [the longest x1 9.37 us: on_device(): arrived = lax.all_to_all(pieces, PLANE, 0, 0, tiled=True)]
    ppermute x9 -> x10, waiting for transfers between devices: 23.2 us -> 35.9 us  [the longest x3 23 us: hop(): return lax.ppermute(mine, ('y', 'c'), pairs)]
    reshape x5 -> x0, local copies, waits for them, and re-layouts: 12.3 us -> none  [the longest x2 4.7 us: on_device(): attended.reshape(blocks, n_x, n_y, n_c, PIECE, cols)]
    ppermute x9 -> x10, starting transfers between devices: 18.2 us -> 26.9 us  [the longest x4 12.6 us: on_device(): parts += [part, lax.ppermute(part, 'c', [(0, 1), (1, 0)])]]
    transpose x1 -> x0, local copies, waits for them, and re-layouts: 4.83 us -> none  [on_device(): home.reshape(n_y, n_x, n_c, n_y * n_c * PIECE, n_x, -1)]
    all_to_all x1 -> x2, waiting for transfers between devices: 38 us -> 41.8 us  [the longest x1 27.1 us: on_device(): arrived = lax.all_to_all(pieces, PLANE, 0, 0, tiled=True)]
    unnamed x12 -> x14, local copies, waits for them, and re-layouts: 4.37 us -> 0.72 us
  transfers between devices with their start and end apart: 11 -> 14, of which waited for: 4 -> 7; matrix products, arithmetic and copies ran while one was open for 4% -> 1% of each run, Pallas kernels for 1% -> 5%
where the time goes in v2:
time: 210 us; the launch traced here: 209 us
  waiting for transfers between devices  78.4 us (37%)
  starting transfers between devices  44.7 us (21%)
  blocking collectives  33.3 us (16%)
  Pallas kernels  31.7 us (15%)
  between operations  13.5 us (6%)
  local copies, waits for them, and re-layouts  6.8 us (3%)
    all_to_all x1, blocking collectives, on_device(): return arrange(lax.all_to_all(projected, PLANE, 0, 0, tiled=True))  33.3 us
    all_to_all x1, waiting for transfers between devices, on_device(): arrived = lax.all_to_all(pieces, PLANE, 0, 0, tiled=True)  27.1 us
    ppermute x3, waiting for transfers between devices, hop(): return lax.ppermute(mine, ('y', 'c'), pairs)  23 us
    pallas_call x1, Pallas kernels, project(): pl.pallas_call(project_kernel, out_shape=jax.ShapeDtypeStruct((groups, 8...  16.7 us
    all_to_all x1, waiting for transfers between devices, on_device(): lax.all_to_all(live.reshape(n_z, groups * PIECE, cols), 'z', 0, 0, tiled=...  14.6 us
    ppermute x4, starting transfers between devices, on_device(): parts += [part, lax.ppermute(part, 'c', [(0, 1), (1, 0)])]  12.6 us
    pallas_call x1, Pallas kernels, attention(): pl.pallas_call(attention_kernel, out_shape=jax.ShapeDtypeStruct((groups,...  11.2 us
    all_to_all x1, starting transfers between devices, on_device(): arrived = lax.all_to_all(pieces, PLANE, 0, 0, tiled=True)  9.37 us
  transfers between devices with their start and end apart: 14, of which 7 were waited for; matrix products, arithmetic and copies ran while one was open for 1% of the time, Pallas kernels for 5%

profile of v2, /device:TPU:1, one launch (start us, length us, event | category | flops | bytes accessed | tf_op | source)
XLA Modules:
  0.0 209.4 jit_solution(3445167378409481468)
XLA Ops:
  6.5 0.7 all-gather.5.cloned.1.call-update
  7.3 11.2 %attention.1 = bf16[32,64,512]{2,1,0:T(8,128)(2,1)} custom-call(s32[2048]{0:T(1024)} %seg_s.1, bf16[2048,512]{1,0:T(8,128)(2,1)} %q_ref.1, bf16[2048,128]{1,0:T(8,128)(2,1)} %k_ref.1, bf16[2048,128]{1,0:T(8,128)(2,1)} %v_ref.1, s32[1,2048]{1,0:T(1,128)} %bitcast.16), custom_call_target="tpu_custom_call" | custom-call | flops 4294967296 | bytes 6291456 | tf_op jit(solution)/shard_map/attention/pallas_call | solution.py:84
  18.5 9.4 %all-to-all-start = ((bf16[32,64,512]{2,1,0:T(8,128)(2,1)}), bf16[32,64,512]{2,1,0:T(8,128)(2,1)S(1)}, u32[]{:S(2)}, u32[]{:S(2)}) async-start(bf16[32,64,512]{2,1,0:T(8,128)(2,1)} %attention.1), calls=%async_computation | async-start | bytes 4194304 | tf_op jit(solution)/shard_map/all_to_all | solution.py:220
  28.5 27.1 %all-to-all-done = bf16[32,64,512]{2,1,0:T(8,128)(2,1)S(1)} async-done(((bf16[32,64,512]{2,1,0:T(8,128)(2,1)}), bf16[32,64,512]{2,1,0:T(8,128)(2,1)S(1)}, u32[]{:S(2)}, u32[]{:S(2)}) %all-to-all-start) | async-done | bytes 2097184 | tf_op jit(solution)/shard_map/all_to_all | solution.py:220
  55.6 5.1 %gather_fusion.1 = bf16[1024,512]{1,0:T(8,128)(2,1)} fusion(bf16[2048,512]{1,0:T(8,128)(2,1)S(1)} %bitcast.9, s32[1024]{0:T(1024)S(1)} %broadcast_clamp_fusion), kind=kCustom, calls=%fused_computation.1 | custom fusion | bytes 2101248 | tf_op jit(solution)/shard_map/jit(_take)/gather | solution.py:229
  60.7 8.3 %all-to-all-start.1 = ((bf16[8,128,512]{2,1,0:T(8,128)(2,1)}), bf16[8,128,512]{2,1,0:T(8,128)(2,1)S(1)}, u32[]{:S(2)}, u32[]{:S(2)}) async-start(bf16[8,128,512]{2,1,0:T(8,128)(2,1)} %bitcast.5), calls=%async_computation.1 | async-start | bytes 2097152 | tf_op jit(solution)/shard_map/all_to_all | solution.py:230
  69.1 1.7 collective-permute-start.9
  70.8 5.2 %collective-permute-done.9 = bf16[512,256]{1,0:T(8,128)(2,1)S(1)} collective-permute-done((bf16[512,256]{1,0:T(8,128)(2,1)S(1)}, bf16[512,256]{1,0:T(8,128)(2,1)S(1)}, u32[]{:S(2)}, u32[]{:S(2)}) %collective-permute-start.9) | collective-permute-done | bytes 262176 | tf_op jit(solution)/shard_map/ppermute | solution.py:217
  75.9 0.7 copy-done.3
  76.6 4.9 %collective-permute-start.8 = (bf16[8,512,256]{2,1,0:T(8,128)(2,1)}, bf16[8,512,256]{2,1,0:T(8,128)(2,1)S(1)}, u32[]{:S(2)}, u32[]{:S(2)}) collective-permute-start(bf16[8,512,256]{2,1,0:T(8,128)(2,1)} %bitcast.12), channel_id=1, source_target_pairs={{0,48},{16,0},{32,16},{48,32},{1,49},{17,1},{33,17},{49,33},{2,50}... | collective-permute-start | bytes 6291464 | tf_op jit(solution)/shard_map/ppermute | solution.py:222
  81.6 14.6 %all-to-all-done.1.refs_0_ = bf16[8,128,512]{2,1,0:T(8,128)(2,1)S(1)} async-done(((bf16[8,128,512]{2,1,0:T(8,128)(2,1)}), bf16[8,128,512]{2,1,0:T(8,128)(2,1)S(1)}, u32[]{:S(2)}, u32[]{:S(2)}) %all-to-all-start.1) | async-done | bytes 1048608 | tf_op jit(solution)/shard_map/all_to_all | solution.py:230
  96.2 2.5 %collective-permute-start.1 = (bf16[8,128,512]{2,1,0:T(8,128)(2,1)S(1)}, bf16[8,128,512]{2,1,0:T(8,128)(2,1)}, u32[]{:S(2)}, u32[]{:S(2)}) collective-permute-start(bf16[8,128,512]{2,1,0:T(8,128)(2,1)S(1)} %all-to-all-done.1.refs_0_), channel_id=1, source_target_pairs={{0,64},{8,200},{64,128},{72,8},{128,192},{136,72},{192,0},{200,136... | collective-permute-start | bytes 3145736 | tf_op jit(solution)/shard_map/ppermute | solution.py:209
  98.7 1.7 collective-permute-start.7
  100.4 17.4 %collective-permute-done.1.refs_2_ = bf16[8,128,512]{2,1,0:T(8,128)(2,1)} collective-permute-done((bf16[8,128,512]{2,1,0:T(8,128)(2,1)S(1)}, bf16[8,128,512]{2,1,0:T(8,128)(2,1)}, u32[]{:S(2)}, u32[]{:S(2)}) %collective-permute-start.1) | collective-permute-done | bytes 1048608 | tf_op jit(solution)/shard_map/ppermute | solution.py:209
  117.8 3.5 %collective-permute-start.5 = (bf16[8,128,512]{2,1,0:T(8,128)(2,1)}, bf16[8,128,512]{2,1,0:T(8,128)(2,1)}, u32[]{:S(2)}, u32[]{:S(2)}) collective-permute-start(bf16[8,128,512]{2,1,0:T(8,128)(2,1)} %collective-permute-done.1.refs_2_), channel_id=1, source_target_pairs={{0,64},{8,200},{64,128},{72,8},{128,192},{136,72},{192,0},{200,136... | collective-permute-start | bytes 3145736 | tf_op jit(solution)/shard_map/ppermute | solution.py:209
  121.3 3.7 %collective-permute-start = (bf16[8,128,512]{2,1,0:T(8,128)(2,1)S(1)}, bf16[8,128,512]{2,1,0:T(8,128)(2,1)}, u32[]{:S(2)}, u32[]{:S(2)}) collective-permute-start(bf16[8,128,512]{2,1,0:T(8,128)(2,1)S(1)} %all-to-all-done.1.refs_0_), channel_id=1, source_target_pairs={{0,8},{8,0},{1,9},{9,1},{2,10},{10,2},{3,11},{11,3},{4,12},{12,4},... | collective-permute-start | bytes 3145736 | tf_op jit(solution)/shard_map/ppermute | solution.py:234
  125.1 1.8 collective-permute-done.8.refs_10_
  126.9 0.8 collective-permute-start.2
  127.8 5.6 %collective-permute-done.5.refs_6_ = bf16[8,128,512]{2,1,0:T(8,128)(2,1)} collective-permute-done((bf16[8,128,512]{2,1,0:T(8,128)(2,1)}, bf16[8,128,512]{2,1,0:T(8,128)(2,1)}, u32[]{:S(2)}, u32[]{:S(2)}) %collective-permute-start.5) | collective-permute-done | bytes 1048608 | tf_op jit(solution)/shard_map/ppermute | solution.py:209
  133.4 8.0 %collective-permute-start.6 = (bf16[8,128,512]{2,1,0:T(8,128)(2,1)}, bf16[8,128,512]{2,1,0:T(8,128)(2,1)}, u32[]{:S(2)}, u32[]{:S(2)}) collective-permute-start(bf16[8,128,512]{2,1,0:T(8,128)(2,1)} %collective-permute-done.5.refs_6_), channel_id=1, source_target_pairs={{0,8},{8,0},{1,9},{9,1},{2,10},{10,2},{3,11},{11,3},{4,12},{12,4},... | collective-permute-start | bytes 3145736 | tf_op jit(solution)/shard_map/ppermute | solution.py:234
  142.7 5.9 %collective-permute-done.7.refs_9_ = bf16[8,512,256]{2,1,0:T(8,128)(2,1)} collective-permute-done((bf16[8,512,256]{2,1,0:T(8,128)(2,1)}, bf16[8,512,256]{2,1,0:T(8,128)(2,1)}, u32[]{:S(2)}, u32[]{:S(2)}) %collective-permute-start.7) | collective-permute-done | bytes 2097184 | tf_op jit(solution)/shard_map/ppermute | solution.py:222
  148.7 16.7 %project.1 = bf16[32,32,1024]{2,1,0:T(8,128)(2,1)} custom-call(s32[12]{0:T(128)} %pad_add_fusion.order_s, bf16[8,128,512]{2,1,0:T(8,128)(2,1)} %copy-done.1, bf16[8,128,512]{2,1,0:T(8,128)(2,1)} %collective-permute-done.refs_1_, bf16[8,128,512]{2,1,0:T(8,128)(2,1)} %collective-permute-done.1.refs_2_, bf16[8,128,512]{2,1,0:T(8,128)(2,1)} %collective-permute-done.2.refs_3_, ...), custom_call_target="tpu_custom_call" | custom-call | flops 8589934592 | bytes 18874368 | tf_op jit(solution)/shard_map/project/pallas_call | solution.py:154
  165.5 33.3 %all_to_all.15 = bf16[32,32,1024]{2,1,0:T(8,128)(2,1)} all-to-all(bf16[32,32,1024]{2,1,0:T(8,128)(2,1)} %project.1), channel_id=1, replica_groups=mesh['y'=4,'x'=4,'c'=2,'z'=8] {'y','x','c'}, dimensions={0} | all-to-all | bytes 4194304 | tf_op jit(solution)/shard_map/all_to_all | solution.py:241
  198.8 3.8 %arrange.1 = bf16[128,8192]{1,0:T(8,128)(2,1)} custom-call(bf16[4,4,2,32,1024]{4,3,2,1,0:T(8,128)(2,1)} %bitcast.10), custom_call_target="tpu_custom_call" | custom-call | bytes 4194304 | tf_op jit(solution)/shard_map/arrange/pallas_call | solution.py:190
  (38 shorter events, 2.1 us)
Async XLA Ops:
  6.5 49.1 %all-gather.5.cloned.1.call-start = ((), (), s32[]{:S(2)}) async-start(), calls=%async_computation.3 | async-start | bytes 2359296 | tf_op jit(solution)/shard_map/all_gather | solution.py:218
  18.5 9.4 %copy-start.4 = (s32[512]{0:T(512)S(1)}, s32[512]{0:T(512)}, u32[]{:S(2)}) copy-start(s32[512]{0:T(512)} %param.13) | copy-start | bytes 6148
  18.5 37.1 %all-to-all-start = ((bf16[32,64,512]{2,1,0:T(8,128)(2,1)}), bf16[32,64,512]{2,1,0:T(8,128)(2,1)S(1)}, u32[]{:S(2)}, u32[]{:S(2)}) async-start(bf16[32,64,512]{2,1,0:T(8,128)(2,1)} %attention.1), calls=%async_computation | async-start | bytes 4194304 | tf_op jit(solution)/shard_map/all_to_all | solution.py:220
  60.7 8.4 %copy-start.2 = (bf16[512,256]{1,0:T(8,128)(2,1)S(1)}, bf16[512,256]{1,0:T(8,128)(2,1)}, u32[]{:S(2)}) copy-start(bf16[512,256]{1,0:T(8,128)(2,1)} %param.11) | copy-start | bytes 786436
  60.7 80.7 %copy-start = (s32[2,4]{1,0:T(2,128)S(1)}, s32[2,4]{1,0:T(2,128)}, u32[]{:S(2)}) copy-start(s32[2,4]{1,0:T(2,128)} %constant.83.clone) | copy-start | bytes 100
  60.7 81.4 %copy-start.6 = (s32[4]{0:T(128)S(1)}, s32[4]{0:T(128)}, u32[]{:S(2)}) copy-start(s32[4]{0:T(128)} %constant.84.clone) | copy-start | bytes 52
  60.7 35.5 %all-to-all-start.1 = ((bf16[8,128,512]{2,1,0:T(8,128)(2,1)}), bf16[8,128,512]{2,1,0:T(8,128)(2,1)S(1)}, u32[]{:S(2)}, u32[]{:S(2)}) async-start(bf16[8,128,512]{2,1,0:T(8,128)(2,1)} %bitcast.5), calls=%async_computation.1 | async-start | bytes 2097152 | tf_op jit(solution)/shard_map/all_to_all | solution.py:230
  69.0 73.7 %all-gather.7.cloned.1.call-start = ((), (), s32[]{:S(2)}) async-start(), calls=%async_computation.4 | async-start | bytes 2359296 | tf_op jit(solution)/shard_map/all_gather | solution.py:217
  69.1 6.8 %collective-permute-start.9 = (bf16[512,256]{1,0:T(8,128)(2,1)S(1)}, bf16[512,256]{1,0:T(8,128)(2,1)S(1)}, u32[]{:S(2)}, u32[]{:S(2)}) collective-permute-start(bf16[512,256]{1,0:T(8,128)(2,1)S(1)} %copy-done.2), channel_id=1, source_target_pairs={{0,32},{16,48},{32,0},{48,16},{1,33},{17,49},{33,1},{49,17},{2,34}... | collective-permute-start | bytes 786440 | tf_op jit(solution)/shard_map/ppermute | solution.py:217
  75.9 0.7 copy-start.3
  76.6 50.3 %collective-permute-start.8 = (bf16[8,512,256]{2,1,0:T(8,128)(2,1)}, bf16[8,512,256]{2,1,0:T(8,128)(2,1)S(1)}, u32[]{:S(2)}, u32[]{:S(2)}) collective-permute-start(bf16[8,512,256]{2,1,0:T(8,128)(2,1)} %bitcast.12), channel_id=1, source_target_pairs={{0,48},{16,0},{32,16},{48,32},{1,49},{17,1},{33,17},{49,33},{2,50}... | collective-permute-start | bytes 6291464 | tf_op jit(solution)/shard_map/ppermute | solution.py:222
  96.2 52.5 %copy-start.1 = (bf16[8,128,512]{2,1,0:T(8,128)(2,1)}, bf16[8,128,512]{2,1,0:T(8,128)(2,1)S(1)}, u32[]{:S(2)}) copy-start(bf16[8,128,512]{2,1,0:T(8,128)(2,1)S(1)} %all-to-all-done.1.refs_0_) | copy-start | bytes 3145732
  96.2 21.6 %collective-permute-start.1 = (bf16[8,128,512]{2,1,0:T(8,128)(2,1)S(1)}, bf16[8,128,512]{2,1,0:T(8,128)(2,1)}, u32[]{:S(2)}, u32[]{:S(2)}) collective-permute-start(bf16[8,128,512]{2,1,0:T(8,128)(2,1)S(1)} %all-to-all-done.1.refs_0_), channel_id=1, source_target_pairs={{0,64},{8,200},{64,128},{72,8},{128,192},{136,72},{192,0},{200,136... | collective-permute-start | bytes 3145736 | tf_op jit(solution)/shard_map/ppermute | solution.py:209
  98.7 49.9 %collective-permute-start.7 = (bf16[8,512,256]{2,1,0:T(8,128)(2,1)}, bf16[8,512,256]{2,1,0:T(8,128)(2,1)}, u32[]{:S(2)}, u32[]{:S(2)}) collective-permute-start(bf16[8,512,256]{2,1,0:T(8,128)(2,1)} %bitcast.13), channel_id=1, source_target_pairs={{0,16},{16,32},{32,48},{48,0},{1,17},{17,33},{33,49},{49,1},{2,18}... | collective-permute-start | bytes 6291464 | tf_op jit(solution)/shard_map/ppermute | solution.py:222
  100.4 27.3 %collective-permute-start.3 = (bf16[8,128,512]{2,1,0:T(8,128)(2,1)S(1)}, bf16[8,128,512]{2,1,0:T(8,128)(2,1)}, u32[]{:S(2)}, u32[]{:S(2)}) collective-permute-start(bf16[8,128,512]{2,1,0:T(8,128)(2,1)S(1)} %all-to-all-done.1.refs_0_), channel_id=1, source_target_pairs={{0,192},{8,72},{64,0},{72,136},{128,64},{136,200},{192,128},{200,8... | collective-permute-start | bytes 3145736 | tf_op jit(solution)/shard_map/ppermute | solution.py:209
  117.8 15.6 %collective-permute-start.5 = (bf16[8,128,512]{2,1,0:T(8,128)(2,1)}, bf16[8,128,512]{2,1,0:T(8,128)(2,1)}, u32[]{:S(2)}, u32[]{:S(2)}) collective-permute-start(bf16[8,128,512]{2,1,0:T(8,128)(2,1)} %collective-permute-done.1.refs_2_), channel_id=1, source_target_pairs={{0,64},{8,200},{64,128},{72,8},{128,192},{136,72},{192,0},{200,136... | collective-permute-start | bytes 3145736 | tf_op jit(solution)/shard_map/ppermute | solution.py:209
  121.3 27.4 %collective-permute-start = (bf16[8,128,512]{2,1,0:T(8,128)(2,1)S(1)}, bf16[8,128,512]{2,1,0:T(8,128)(2,1)}, u32[]{:S(2)}, u32[]{:S(2)}) collective-permute-start(bf16[8,128,512]{2,1,0:T(8,128)(2,1)S(1)} %all-to-all-done.1.refs_0_), channel_id=1, source_target_pairs={{0,8},{8,0},{1,9},{9,1},{2,10},{10,2},{3,11},{11,3},{4,12},{12,4},... | collective-permute-start | bytes 3145736 | tf_op jit(solution)/shard_map/ppermute | solution.py:234
  126.9 21.8 %copy-start.5 = (bf16[8,512,256]{2,1,0:T(8,128)(2,1)}, bf16[8,512,256]{2,1,0:T(8,128)(2,1)S(1)}, u32[]{:S(2)}) copy-start(bf16[8,512,256]{2,1,0:T(8,128)(2,1)S(1)} %collective-permute-done.8.refs_10_) | copy-start | bytes 6291460
  126.9 21.8 %collective-permute-start.2 = (bf16[8,128,512]{2,1,0:T(8,128)(2,1)}, bf16[8,128,512]{2,1,0:T(8,128)(2,1)}, u32[]{:S(2)}, u32[]{:S(2)}) collective-permute-start(bf16[8,128,512]{2,1,0:T(8,128)(2,1)} %collective-permute-done.1.refs_2_), channel_id=1, source_target_pairs={{0,8},{8,0},{1,9},{9,1},{2,10},{10,2},{3,11},{11,3},{4,12},{12,4},... | collective-permute-start | bytes 3145736 | tf_op jit(solution)/shard_map/ppermute | solution.py:234
  127.7 21.0 %collective-permute-start.4 = (bf16[8,128,512]{2,1,0:T(8,128)(2,1)}, bf16[8,128,512]{2,1,0:T(8,128)(2,1)}, u32[]{:S(2)}, u32[]{:S(2)}) collective-permute-start(bf16[8,128,512]{2,1,0:T(8,128)(2,1)} %collective-permute-done.3.refs_4_), channel_id=1, source_target_pairs={{0,8},{8,0},{1,9},{9,1},{2,10},{10,2},{3,11},{11,3},{4,12},{12,4},... | collective-permute-start | bytes 3145736 | tf_op jit(solution)/shard_map/ppermute | solution.py:234
  133.4 15.3 %collective-permute-start.6 = (bf16[8,128,512]{2,1,0:T(8,128)(2,1)}, bf16[8,128,512]{2,1,0:T(8,128)(2,1)}, u32[]{:S(2)}, u32[]{:S(2)}) collective-permute-start(bf16[8,128,512]{2,1,0:T(8,128)(2,1)} %collective-permute-done.5.refs_6_), channel_id=1, source_target_pairs={{0,8},{8,0},{1,9},{9,1},{2,10},{10,2},{3,11},{11,3},{4,12},{12,4},... | collective-permute-start | bytes 3145736 | tf_op jit(solution)/shard_map/ppermute | solution.py:234
Sparse Core Ops, SparseCore 0:
  9.1 41.3 all-gather.4
  76.8 41.7 all-gather.6

commit v3 on v2

--- a/solution.py
+++ b/solution.py
@@ -110,7 +110,8 @@
 
     def row_copy(k, z):
         into = rows_scr.at[pl.ds(k * BLOCK, BLOCK), pl.ds(z * depth, depth)]
-        return pltpu.make_async_copy(parts[k].at[z], into, row_sems.at[k * sets + z])
+        source = parts[k].at[lax.rem(order_s[12] + sets - z, sets)]
+        return pltpu.make_async_copy(source, into, row_sems.at[k * sets + z])
 
     def weight_copy(k):
         return pltpu.make_async_copy(weights[k], w_scr.at[k], w_sems.at[k])
@@ -203,23 +204,66 @@
     return [(i, (i + apart) % n) for i in range(n)]
 
 
-def hop(mine, turn):
-    n_y, n_c = lax.axis_size("y"), lax.axis_size("c")
-    pairs = [(y * n_c + c, (y + turn * (1 - 2 * c)) % n_y * n_c + c) for y in range(n_y) for c in range(n_c)]
-    return lax.ppermute(mine, ("y", "c"), pairs)
+def join_kernel(*refs):
+    *sources, o_ref, held, in_sems, out_sems = refs
+    fetch = [pltpu.make_async_copy(source, held.at[k], in_sems.at[k]) for k, source in enumerate(sources)]
+    store = [pltpu.make_async_copy(held.at[k], o_ref.at[k], out_sems.at[k]) for k in range(len(sources))]
+    for copy in fetch:
+        copy.start()
+    for arriving, leaving in zip(fetch, store):
+        arriving.wait()
+        leaving.start()
+    for copy in store:
+        copy.wait()
+
+
+def join(shards):
+    n = len(shards)
+    return pl.pallas_call(
+        join_kernel,
+        out_shape=jax.ShapeDtypeStruct((n, *shards[0].shape), shards[0].dtype),
+        in_specs=[pl.BlockSpec(memory_space=pl.ANY)] * n,
+        out_specs=pl.BlockSpec(memory_space=pl.ANY),
+        scratch_shapes=[
+            pltpu.VMEM((n, *shards[0].shape), shards[0].dtype),
+            pltpu.SemaphoreType.DMA((n,)),
+            pltpu.SemaphoreType.DMA((n,)),
+        ],
+        compiler_params=pltpu.CompilerParams(vmem_limit_bytes=56 * MB),
+        cost_estimate=pl.CostEstimate(flops=0, bytes_accessed=4 * MB, transcendentals=0),
+        name="join",
+    )(*shards)
+
+
+def ring(shard, before, after, axis):
+    n = lax.axis_size(axis)
+    before, after = [shard, before], [after]
+    for _ in range(n // 2 - 1):
+        before.append(lax.ppermute(before[-1], axis, neighbours(axis, n, 1)))
+    for _ in range(n - n // 2 - 2):
+        after.append(lax.ppermute(after[-1], axis, neighbours(axis, n, -1)))
+    return before + after[::-1]
+
+
+def hop(mine, axis, turn):
+    n, n_c = lax.axis_size(axis), lax.axis_size("c")
+    pairs = [(i * n_c + c, (i + turn * (1 - 2 * c)) % n * n_c + c) for i in range(n) for c in range(n_c)]
+    return lax.ppermute(mine, (axis, "c"), pairs)
 
 
 def on_device(queries, keys, values, out_weight, segments, send_plan):
     n_y, n_x, n_c, n_z = (lax.axis_size(a) for a in ("y", "x", "c", "z"))
+    my_y, my_x, my_c = (lax.axis_index(a) for a in PLANE)
     groups = n_y * n_x * n_c
     rows, cols = queries.shape
     blocks = rows // BLOCK
-    w_across = lax.all_gather(lax.ppermute(out_weight, "x", neighbours("x", n_x, 2)), "z")
-    w_own = lax.all_gather(out_weight, "z")
+    z_before, z_after = (lax.ppermute(out_weight, "z", neighbours("z", n_z, turn)) for turn in (1, -1))
     pieces = attention(queries, keys, values, segments)
+    z_before, z_after, pieces = lax.optimization_barrier((z_before, z_after, pieces))
     arrived = lax.all_to_all(pieces, PLANE, 0, 0, tiled=True)
-    w_own, arrived = lax.optimization_barrier((w_own, arrived))
-    w_below, w_above = (lax.ppermute(w_own, "x", neighbours("x", n_x, turn)) for turn in (1, -1))
+    shards, arrived = lax.optimization_barrier((ring(out_weight, z_before, z_after, "z"), arrived))
+    w_own = join(shards)
+    w_ahead, w_behind = hop(w_own, "x", 1), hop(w_own, "x", -1)
     slots = jnp.arange(groups * BAL)
     block_of = jnp.sum(
         jnp.where(send_plan[None, :] == slots[:, None], jnp.arange(groups * blocks)[None, :], 0), axis=1, dtype=jnp.int32
@@ -228,16 +272,19 @@
     row_of = (block_of[:, None] * PIECE + jnp.arange(PIECE)[None, :]).reshape(-1)
     live = jnp.take(arrived.reshape(groups * blocks * PIECE, cols), row_of, axis=0, mode="clip")
     mine = lax.all_to_all(live.reshape(n_z, groups * PIECE, cols), "z", 0, 0, tiled=True)
-    ahead, behind = hop(mine, 1), hop(mine, -1)
+    ahead = hop(mine, "y", 1)
+    w_ahead, ahead, mine = lax.optimization_barrier((w_ahead, ahead, mine))
+    w_across, behind = hop(w_ahead, "x", 1), hop(mine, "y", -1)
     parts = []
-    for part in (mine, ahead, behind, hop(ahead, 1)):
+    for part in (mine, ahead, behind, hop(ahead, "y", 1)):
         parts += [part, lax.ppermute(part, "c", [(0, 1), (1, 0)])]
-    my_y, my_x, my_c = (lax.axis_index(a) for a in PLANE)
     from_y, from_c = jnp.divmod(jnp.arange(n_y * n_c), n_c)
     place = jnp.array([[0, 2, 6, 4], [0, 4, 6, 2]], jnp.int32)
     order = place[from_c, (my_y - from_y) % n_y] + (my_c != from_c)
-    order = jnp.concatenate([order, (my_x + jnp.array([0, 3, 1, 2], jnp.int32)) % n_x])
-    projected = project(order.astype(jnp.int32), parts, (w_own, w_below, w_above, w_across))
+    turn = 1 - 2 * my_c
+    from_x = (my_x - turn * jnp.array([0, 1, -1, 2])) % n_x
+    order = jnp.concatenate([order, from_x, lax.axis_index("z").reshape(1)])
+    projected = project(order.astype(jnp.int32), parts, (w_own, w_ahead, w_behind, w_across))
     return arrange(lax.all_to_all(projected, PLANE, 0, 0, tiled=True))
 
 

time: 210 us -> 203 us (0.967)
  between operations: 13.5 us -> 0.18 us
  starting transfers between devices: 44.7 us -> 51.6 us
  waiting for transfers between devices: 78.4 us -> 75.8 us
    all_to_all x1, waiting for transfers between devices: 27.1 us -> 3.69 us  [on_device(): arrived = lax.all_to_all(pieces, PLANE, 0, 0, tiled=True)]
    ppermute x6 -> x13, waiting for transfers between devices: 35.9 us -> 47 us  [the longest x6 29.1 us: hop(): return lax.ppermute(mine, (axis, 'c'), pairs)]
    ppermute x6 -> x13, starting transfers between devices: 14.3 us -> 23.9 us  [the longest x6 11.8 us: hop(): return lax.ppermute(mine, (axis, 'c'), pairs)]
    all_to_all x1, waiting for transfers between devices: 14.6 us -> 22.6 us  [on_device(): lax.all_to_all(live.reshape(n_z, groups * PIECE, cols), 'z', 0, 0, tiled=...]
    all_to_all x1, starting transfers between devices: 9.37 us -> 12.7 us  [on_device(): arrived = lax.all_to_all(pieces, PLANE, 0, 0, tiled=True)]
    ppermute x4, starting transfers between devices: 12.6 us -> 9.41 us  [on_device(): parts += [part, lax.ppermute(part, 'c', [(0, 1), (1, 0)])]]
    all_to_all x1, starting transfers between devices: 8.33 us -> 5.57 us  [on_device(): lax.all_to_all(live.reshape(n_z, groups * PIECE, cols), 'z', 0, 0, tiled=...]
    ppermute x4, waiting for transfers between devices: 0.01 us -> 2.51 us  [on_device(): parts += [part, lax.ppermute(part, 'c', [(0, 1), (1, 0)])]]
  transfers between devices with their start and end apart: 14 -> 19, of which waited for: 7 -> 10; matrix products, arithmetic and copies ran while one was open for 1% -> 1% of each run, Pallas kernels for 5% -> 6%
where the time goes in v3:
time: 203 us
  waiting for transfers between devices  75.8 us (37%)
  starting transfers between devices  51.6 us (25%)
  blocking collectives  35 us (17%)
  Pallas kernels  33.3 us (16%)
  local copies, waits for them, and re-layouts  6.13 us (3%)
    all_to_all x1, blocking collectives, on_device(): return arrange(lax.all_to_all(projected, PLANE, 0, 0, tiled=True))  35 us
    ppermute x6, waiting for transfers between devices, hop(): return lax.ppermute(mine, (axis, 'c'), pairs)  29.1 us
    all_to_all x1, waiting for transfers between devices, on_device(): lax.all_to_all(live.reshape(n_z, groups * PIECE, cols), 'z', 0, 0, tiled=...  22.6 us
    ppermute x3, waiting for transfers between devices, ring(): before.append(lax.ppermute(before[-1], axis, neighbours(axis, n, 1)))  17.8 us
    pallas_call x1, Pallas kernels, project(): pl.pallas_call(project_kernel, out_shape=jax.ShapeDtypeStruct((groups, 8...  16.7 us
    all_to_all x1, starting transfers between devices, on_device(): arrived = lax.all_to_all(pieces, PLANE, 0, 0, tiled=True)  12.7 us
    ppermute x6, starting transfers between devices, hop(): return lax.ppermute(mine, (axis, 'c'), pairs)  11.8 us
    pallas_call x1, Pallas kernels, attention(): pl.pallas_call(attention_kernel, out_shape=jax.ShapeDtypeStruct((groups,...  10.4 us
  transfers between devices with their start and end apart: 19, of which 10 were waited for; matrix products, arithmetic and copies ran while one was open for 1% of the time, Pallas kernels for 6%

profile of v3, /device:TPU:1, one launch (start us, length us, event | category | flops | bytes accessed | tf_op | source)
XLA Modules:
  0.0 202.9 jit_solution(16018972183170007933)
XLA Ops:
  0.0 2.5 %collective-permute-start = (bf16[512,256]{1,0:T(8,128)(2,1)}, bf16[512,256]{1,0:T(8,128)(2,1)S(1)}, u32[]{:S(2)}, u32[]{:S(2)}) collective-permute-start(bf16[512,256]{1,0:T(8,128)(2,1)} %refs_0_), channel_id=1, source_target_pairs={{0,1},{1,2},{2,3},{3,4},{4,5},{5,6},{6,7},{7,0},{8,9},{9,10},{10,1... | collective-permute-start | bytes 786440 | tf_op jit(solution)/shard_map/ppermute | solution.py:260
  2.5 3.9 %collective-permute-start.1 = (bf16[512,256]{1,0:T(8,128)(2,1)}, bf16[512,256]{1,0:T(8,128)(2,1)S(1)}, u32[]{:S(2)}, u32[]{:S(2)}) collective-permute-start(bf16[512,256]{1,0:T(8,128)(2,1)} %refs_0_), channel_id=1, source_target_pairs={{0,7},{1,0},{2,1},{3,2},{4,3},{5,4},{6,5},{7,6},{8,15},{9,8},{10,9... | collective-permute-start | bytes 786440 | tf_op jit(solution)/shard_map/ppermute | solution.py:260
  6.4 10.4 %attention.1 = bf16[32,64,512]{2,1,0:T(8,128)(2,1)} custom-call(s32[2048]{0:T(1024)} %seg_s.1, bf16[2048,512]{1,0:T(8,128)(2,1)} %q_ref.1, bf16[2048,128]{1,0:T(8,128)(2,1)} %k_ref.1, bf16[2048,128]{1,0:T(8,128)(2,1)} %v_ref.1, s32[1,2048]{1,0:T(1,128)} %bitcast.11), custom_call_target="tpu_custom_call" | custom-call | flops 4294967296 | bytes 6291456 | tf_op jit(solution)/shard_map/attention/pallas_call | solution.py:84
  16.8 12.7 %all-to-all-start = ((bf16[32,64,512]{2,1,0:T(8,128)(2,1)}), bf16[32,64,512]{2,1,0:T(8,128)(2,1)S(1)}, u32[]{:S(2)}, u32[]{:S(2)}) async-start(bf16[32,64,512]{2,1,0:T(8,128)(2,1)} %attention.1), calls=%async_computation | async-start | bytes 4194304 | tf_op jit(solution)/shard_map/all_to_all | solution.py:263
  29.8 2.7 %collective-permute-start.5 = (bf16[512,256]{1,0:T(8,128)(2,1)S(1)}, bf16[512,256]{1,0:T(8,128)(2,1)S(1)}, u32[]{:S(2)}, u32[]{:S(2)}) collective-permute-start(bf16[512,256]{1,0:T(8,128)(2,1)S(1)} %collective-permute-done.1.refs_7_), channel_id=1, source_target_pairs={{0,7},{1,0},{2,1},{3,2},{4,3},{5,4},{6,5},{7,6},{8,15},{9,8},{10,9... | collective-permute-start | bytes 786440 | tf_op jit(solution)/shard_map/ppermute | solution.py:244
  32.5 6.2 %collective-permute-done.2.refs_2_ = bf16[512,256]{1,0:T(8,128)(2,1)S(1)} collective-permute-done((bf16[512,256]{1,0:T(8,128)(2,1)S(1)}, bf16[512,256]{1,0:T(8,128)(2,1)S(1)}, u32[]{:S(2)}, u32[]{:S(2)}) %collective-permute-start.2) | collective-permute-done | bytes 262176 | tf_op jit(solution)/shard_map/ppermute | solution.py:242
  39.1 2.7 %collective-permute-start.6 = (bf16[512,256]{1,0:T(8,128)(2,1)S(1)}, bf16[512,256]{1,0:T(8,128)(2,1)S(1)}, u32[]{:S(2)}, u32[]{:S(2)}) collective-permute-start(bf16[512,256]{1,0:T(8,128)(2,1)S(1)} %collective-permute-done.5.refs_6_), channel_id=1, source_target_pairs={{0,7},{1,0},{2,1},{3,2},{4,3},{5,4},{6,5},{7,6},{8,15},{9,8},{10,9... | collective-permute-start | bytes 786440 | tf_op jit(solution)/shard_map/ppermute | solution.py:244
  41.8 4.8 %collective-permute-done.3.refs_3_ = bf16[512,256]{1,0:T(8,128)(2,1)S(1)} collective-permute-done((bf16[512,256]{1,0:T(8,128)(2,1)S(1)}, bf16[512,256]{1,0:T(8,128)(2,1)S(1)}, u32[]{:S(2)}, u32[]{:S(2)}) %collective-permute-start.3) | collective-permute-done | bytes 262176 | tf_op jit(solution)/shard_map/ppermute | solution.py:242
  46.9 6.8 %collective-permute-done.4.refs_4_ = bf16[512,256]{1,0:T(8,128)(2,1)S(1)} collective-permute-done((bf16[512,256]{1,0:T(8,128)(2,1)S(1)}, bf16[512,256]{1,0:T(8,128)(2,1)S(1)}, u32[]{:S(2)}, u32[]{:S(2)}) %collective-permute-start.4) | collective-permute-done | bytes 262176 | tf_op jit(solution)/shard_map/ppermute | solution.py:242
  53.7 3.7 %all-to-all-done = bf16[32,64,512]{2,1,0:T(8,128)(2,1)S(1)} async-done(((bf16[32,64,512]{2,1,0:T(8,128)(2,1)}), bf16[32,64,512]{2,1,0:T(8,128)(2,1)S(1)}, u32[]{:S(2)}, u32[]{:S(2)}) %all-to-all-start) | async-done | bytes 2097184 | tf_op jit(solution)/shard_map/all_to_all | solution.py:263
  57.4 5.1 %gather_fusion.1 = bf16[1024,512]{1,0:T(8,128)(2,1)} fusion(bf16[2048,512]{1,0:T(8,128)(2,1)S(1)} %bitcast.8, s32[1024]{0:T(1024)S(1)} %broadcast_clamp_fusion), kind=kCustom, calls=%fused_computation.1 | custom fusion | bytes 2101248 | tf_op jit(solution)/shard_map/jit(_take)/gather | solution.py:273
  62.5 5.6 %all-to-all-start.1 = ((bf16[8,128,512]{2,1,0:T(8,128)(2,1)}), bf16[8,128,512]{2,1,0:T(8,128)(2,1)S(1)}, u32[]{:S(2)}, u32[]{:S(2)}) async-start(bf16[8,128,512]{2,1,0:T(8,128)(2,1)} %bitcast.5), calls=%async_computation.1 | async-start | bytes 2097152 | tf_op jit(solution)/shard_map/all_to_all | solution.py:274
  68.1 2.4 %join.1.refs_8_ = bf16[8,512,256]{2,1,0:T(8,128)(2,1)} custom-call(bf16[512,256]{1,0:T(8,128)(2,1)} %refs_0_, bf16[512,256]{1,0:T(8,128)(2,1)} %copy-done.2, bf16[512,256]{1,0:T(8,128)(2,1)} %copy-done.4, bf16[512,256]{1,0:T(8,128)(2,1)} %copy-done.6, bf16[512,256]{1,0:T(8,128)(2,1)} %copy-done.8, bf16[512,256]{1,0:T(8,128)(2,1)} %copy-done.7, ...), custom_call_target="tpu_custom_call" | custom-call | bytes 4194304 | tf_op jit(solution)/shard_map/join/pallas_call | solution.py:222
  72.7 22.6 %all-to-all-done.1.refs_0_ = bf16[8,128,512]{2,1,0:T(8,128)(2,1)S(1)} async-done(((bf16[8,128,512]{2,1,0:T(8,128)(2,1)}), bf16[8,128,512]{2,1,0:T(8,128)(2,1)S(1)}, u32[]{:S(2)}, u32[]{:S(2)}) %all-to-all-start.1) | async-done | bytes 1048608 | tf_op jit(solution)/shard_map/all_to_all | solution.py:274
  95.3 2.5 %collective-permute-start.8 = (bf16[8,128,512]{2,1,0:T(8,128)(2,1)S(1)}, bf16[8,128,512]{2,1,0:T(8,128)(2,1)}, u32[]{:S(2)}, u32[]{:S(2)}) collective-permute-start(bf16[8,128,512]{2,1,0:T(8,128)(2,1)S(1)} %all-to-all-done.1.refs_0_), channel_id=1, source_target_pairs={{0,64},{8,200},{64,128},{72,8},{128,192},{136,72},{192,0},{200,136... | collective-permute-start | bytes 3145736 | tf_op jit(solution)/shard_map/ppermute | solution.py:251
  99.2 11.3 %collective-permute-done.8.refs_2_ = bf16[8,128,512]{2,1,0:T(8,128)(2,1)} collective-permute-done((bf16[8,128,512]{2,1,0:T(8,128)(2,1)S(1)}, bf16[8,128,512]{2,1,0:T(8,128)(2,1)}, u32[]{:S(2)}, u32[]{:S(2)}) %collective-permute-start.8) | collective-permute-done | bytes 1048608 | tf_op jit(solution)/shard_map/ppermute | solution.py:251
  113.2 3.0 %collective-permute-start.16 = (bf16[8,512,256]{2,1,0:T(8,128)(2,1)S(1)}, bf16[8,512,256]{2,1,0:T(8,128)(2,1)}, u32[]{:S(2)}, u32[]{:S(2)}) collective-permute-start(bf16[8,512,256]{2,1,0:T(8,128)(2,1)S(1)} %collective-permute-done.7.refs_9_), channel_id=1, source_target_pairs={{0,16},{8,56},{16,32},{24,8},{32,48},{40,24},{48,0},{56,40},{1,17}... | collective-permute-start | bytes 6291464 | tf_op jit(solution)/shard_map/ppermute | solution.py:251
  116.9 12.6 %collective-permute-done.15.refs_10_ = bf16[8,512,256]{2,1,0:T(8,128)(2,1)S(1)} collective-permute-done((bf16[8,512,256]{2,1,0:T(8,128)(2,1)}, bf16[8,512,256]{2,1,0:T(8,128)(2,1)S(1)}, u32[]{:S(2)}, u32[]{:S(2)}) %collective-permute-start.15) | collective-permute-done | bytes 2097184 | tf_op jit(solution)/shard_map/ppermute | solution.py:251
  129.5 4.0 %collective-permute-start.10 = (bf16[8,128,512]{2,1,0:T(8,128)(2,1)}, bf16[8,128,512]{2,1,0:T(8,128)(2,1)}, u32[]{:S(2)}, u32[]{:S(2)}) collective-permute-start(bf16[8,128,512]{2,1,0:T(8,128)(2,1)} %collective-permute-done.8.refs_2_), channel_id=1, source_target_pairs={{0,8},{8,0},{1,9},{9,1},{2,10},{10,2},{3,11},{11,3},{4,12},{12,4},... | collective-permute-start | bytes 3145736 | tf_op jit(solution)/shard_map/ppermute | solution.py:280
  133.5 4.5 %collective-permute-start.12 = (bf16[8,128,512]{2,1,0:T(8,128)(2,1)}, bf16[8,128,512]{2,1,0:T(8,128)(2,1)}, u32[]{:S(2)}, u32[]{:S(2)}) collective-permute-start(bf16[8,128,512]{2,1,0:T(8,128)(2,1)} %collective-permute-done.11.refs_4_), channel_id=1, source_target_pairs={{0,8},{8,0},{1,9},{9,1},{2,10},{10,2},{3,11},{11,3},{4,12},{12,4},... | collective-permute-start | bytes 3145736 | tf_op jit(solution)/shard_map/ppermute | solution.py:280
  142.1 5.2 %collective-permute-done.16.refs_11_ = bf16[8,512,256]{2,1,0:T(8,128)(2,1)} collective-permute-done((bf16[8,512,256]{2,1,0:T(8,128)(2,1)S(1)}, bf16[8,512,256]{2,1,0:T(8,128)(2,1)}, u32[]{:S(2)}, u32[]{:S(2)}) %collective-permute-start.16) | collective-permute-done | bytes 2097184 | tf_op jit(solution)/shard_map/ppermute | solution.py:251
  147.3 16.7 %project.1 = bf16[32,32,1024]{2,1,0:T(8,128)(2,1)} custom-call(s32[13]{0:T(128)} %pad_add_fusion.order_s, bf16[8,128,512]{2,1,0:T(8,128)(2,1)} %copy-done.1, bf16[8,128,512]{2,1,0:T(8,128)(2,1)} %collective-permute-done.9.refs_1_, bf16[8,128,512]{2,1,0:T(8,128)(2,1)} %collective-permute-done.8.refs_2_, bf16[8,128,512]{2,1,0:T(8,128)(2,1)} %collective-permute-done.10.refs_3_, ...), custom_call_target="tpu_custom_call" | custom-call | flops 8589934592 | bytes 18874368 | tf_op jit(solution)/shard_map/project/pallas_call | solution.py:155
  164.1 35.0 %all_to_all.15 = bf16[32,32,1024]{2,1,0:T(8,128)(2,1)} all-to-all(bf16[32,32,1024]{2,1,0:T(8,128)(2,1)} %project.1), channel_id=1, replica_groups=mesh['y'=4,'x'=4,'c'=2,'z'=8] {'y','x','c'}, dimensions={0} | all-to-all | bytes 4194304 | tf_op jit(solution)/shard_map/all_to_all | solution.py:288
  199.1 3.8 %arrange.1 = bf16[128,8192]{1,0:T(8,128)(2,1)} custom-call(bf16[4,4,2,32,1024]{4,3,2,1,0:T(8,128)(2,1)} %bitcast.9), custom_call_target="tpu_custom_call" | custom-call | bytes 4194304 | tf_op jit(solution)/shard_map/arrange/pallas_call | solution.py:191
  (59 shorter events, 12.0 us)
Async XLA Ops:
  0.0 16.8 %collective-permute-start = (bf16[512,256]{1,0:T(8,128)(2,1)}, bf16[512,256]{1,0:T(8,128)(2,1)S(1)}, u32[]{:S(2)}, u32[]{:S(2)}) collective-permute-start(bf16[512,256]{1,0:T(8,128)(2,1)} %refs_0_), channel_id=1, source_target_pairs={{0,1},{1,2},{2,3},{3,4},{4,5},{5,6},{6,7},{7,0},{8,9},{9,10},{10,1... | collective-permute-start | bytes 786440 | tf_op jit(solution)/shard_map/ppermute | solution.py:260
  2.5 14.4 %collective-permute-start.1 = (bf16[512,256]{1,0:T(8,128)(2,1)}, bf16[512,256]{1,0:T(8,128)(2,1)S(1)}, u32[]{:S(2)}, u32[]{:S(2)}) collective-permute-start(bf16[512,256]{1,0:T(8,128)(2,1)} %refs_0_), channel_id=1, source_target_pairs={{0,7},{1,0},{2,1},{3,2},{4,3},{5,4},{6,5},{7,6},{8,15},{9,8},{10,9... | collective-permute-start | bytes 786440 | tf_op jit(solution)/shard_map/ppermute | solution.py:260
  16.8 40.5 %all-to-all-start = ((bf16[32,64,512]{2,1,0:T(8,128)(2,1)}), bf16[32,64,512]{2,1,0:T(8,128)(2,1)S(1)}, u32[]{:S(2)}, u32[]{:S(2)}) async-start(bf16[32,64,512]{2,1,0:T(8,128)(2,1)} %attention.1), calls=%async_computation | async-start | bytes 4194304 | tf_op jit(solution)/shard_map/all_to_all | solution.py:263
  29.5 9.1 %collective-permute-start.2 = (bf16[512,256]{1,0:T(8,128)(2,1)S(1)}, bf16[512,256]{1,0:T(8,128)(2,1)S(1)}, u32[]{:S(2)}, u32[]{:S(2)}) collective-permute-start(bf16[512,256]{1,0:T(8,128)(2,1)S(1)} %collective-permute-done.refs_1_), channel_id=1, source_target_pairs={{0,1},{1,2},{2,3},{3,4},{4,5},{5,6},{6,7},{7,0},{8,9},{9,10},{10,1... | collective-permute-start | bytes 786440 | tf_op jit(solution)/shard_map/ppermute | solution.py:242
  29.8 9.3 %collective-permute-start.5 = (bf16[512,256]{1,0:T(8,128)(2,1)S(1)}, bf16[512,256]{1,0:T(8,128)(2,1)S(1)}, u32[]{:S(2)}, u32[]{:S(2)}) collective-permute-start(bf16[512,256]{1,0:T(8,128)(2,1)S(1)} %collective-permute-done.1.refs_7_), channel_id=1, source_target_pairs={{0,7},{1,0},{2,1},{3,2},{4,3},{5,4},{6,5},{7,6},{8,15},{9,8},{10,9... | collective-permute-start | bytes 786440 | tf_op jit(solution)/shard_map/ppermute | solution.py:244
  38.7 23.8 %copy-start.4 = (bf16[512,256]{1,0:T(8,128)(2,1)}, bf16[512,256]{1,0:T(8,128)(2,1)S(1)}, u32[]{:S(2)}) copy-start(bf16[512,256]{1,0:T(8,128)(2,1)S(1)} %collective-permute-done.2.refs_2_) | copy-start | bytes 786436
  38.7 8.0 %collective-permute-start.3 = (bf16[512,256]{1,0:T(8,128)(2,1)S(1)}, bf16[512,256]{1,0:T(8,128)(2,1)S(1)}, u32[]{:S(2)}, u32[]{:S(2)}) collective-permute-start(bf16[512,256]{1,0:T(8,128)(2,1)S(1)} %collective-permute-done.2.refs_2_), channel_id=1, source_target_pairs={{0,1},{1,2},{2,3},{3,4},{4,5},{5,6},{6,7},{7,0},{8,9},{9,10},{10,1... | collective-permute-start | bytes 786440 | tf_op jit(solution)/shard_map/ppermute | solution.py:242
  39.1 7.8 %collective-permute-start.6 = (bf16[512,256]{1,0:T(8,128)(2,1)S(1)}, bf16[512,256]{1,0:T(8,128)(2,1)S(1)}, u32[]{:S(2)}, u32[]{:S(2)}) collective-permute-start(bf16[512,256]{1,0:T(8,128)(2,1)S(1)} %collective-permute-done.5.refs_6_), channel_id=1, source_target_pairs={{0,7},{1,0},{2,1},{3,2},{4,3},{5,4},{6,5},{7,6},{8,15},{9,8},{10,9... | collective-permute-start | bytes 786440 | tf_op jit(solution)/shard_map/ppermute | solution.py:244
  46.6 7.0 %collective-permute-start.4 = (bf16[512,256]{1,0:T(8,128)(2,1)S(1)}, bf16[512,256]{1,0:T(8,128)(2,1)S(1)}, u32[]{:S(2)}, u32[]{:S(2)}) collective-permute-start(bf16[512,256]{1,0:T(8,128)(2,1)S(1)} %collective-permute-done.3.refs_3_), channel_id=1, source_target_pairs={{0,1},{1,2},{2,3},{3,4},{4,5},{5,6},{6,7},{7,0},{8,9},{9,10},{10,1... | collective-permute-start | bytes 786440 | tf_op jit(solution)/shard_map/ppermute | solution.py:242
  62.5 32.8 %all-to-all-start.1 = ((bf16[8,128,512]{2,1,0:T(8,128)(2,1)}), bf16[8,128,512]{2,1,0:T(8,128)(2,1)S(1)}, u32[]{:S(2)}, u32[]{:S(2)}) async-start(bf16[8,128,512]{2,1,0:T(8,128)(2,1)} %bitcast.5), calls=%async_computation.1 | async-start | bytes 2097152 | tf_op jit(solution)/shard_map/all_to_all | solution.py:274
  68.0 70.3 %copy-start = (s32[2,4]{1,0:T(2,128)S(1)}, s32[2,4]{1,0:T(2,128)}, u32[]{:S(2)}) copy-start(s32[2,4]{1,0:T(2,128)} %constant.87.clone) | copy-start | bytes 100
  68.0 70.9 %copy-start.10 = (s32[4]{0:T(128)S(1)}, s32[4]{0:T(128)}, u32[]{:S(2)}) copy-start(s32[4]{0:T(128)} %constant.88.clone) | copy-start | bytes 52
  70.5 28.8 %collective-permute-start.7 = (bf16[8,512,256]{2,1,0:T(8,128)(2,1)}, bf16[8,512,256]{2,1,0:T(8,128)(2,1)S(1)}, u32[]{:S(2)}, u32[]{:S(2)}) collective-permute-start(bf16[8,512,256]{2,1,0:T(8,128)(2,1)} %join.1.refs_8_), channel_id=1, source_target_pairs={{0,16},{8,56},{16,32},{24,8},{32,48},{40,24},{48,0},{56,40},{1,17}... | collective-permute-start | bytes 6291464 | tf_op jit(solution)/shard_map/ppermute | solution.py:251
  95.3 52.0 %copy-start.1 = (bf16[8,128,512]{2,1,0:T(8,128)(2,1)}, bf16[8,128,512]{2,1,0:T(8,128)(2,1)S(1)}, u32[]{:S(2)}) copy-start(bf16[8,128,512]{2,1,0:T(8,128)(2,1)S(1)} %all-to-all-done.1.refs_0_) | copy-start | bytes 3145732
  95.3 15.3 %collective-permute-start.8 = (bf16[8,128,512]{2,1,0:T(8,128)(2,1)S(1)}, bf16[8,128,512]{2,1,0:T(8,128)(2,1)}, u32[]{:S(2)}, u32[]{:S(2)}) collective-permute-start(bf16[8,128,512]{2,1,0:T(8,128)(2,1)S(1)} %all-to-all-done.1.refs_0_), channel_id=1, source_target_pairs={{0,64},{8,200},{64,128},{72,8},{128,192},{136,72},{192,0},{200,136... | collective-permute-start | bytes 3145736 | tf_op jit(solution)/shard_map/ppermute | solution.py:251
  97.7 31.8 %collective-permute-start.15 = (bf16[8,512,256]{2,1,0:T(8,128)(2,1)}, bf16[8,512,256]{2,1,0:T(8,128)(2,1)S(1)}, u32[]{:S(2)}, u32[]{:S(2)}) collective-permute-start(bf16[8,512,256]{2,1,0:T(8,128)(2,1)} %join.1.refs_8_), channel_id=1, source_target_pairs={{0,48},{8,24},{16,0},{24,40},{32,16},{40,56},{48,32},{56,8},{1,49}... | collective-permute-start | bytes 6291464 | tf_op jit(solution)/shard_map/ppermute | solution.py:251
  99.2 48.1 %copy-start.11 = (bf16[8,512,256]{2,1,0:T(8,128)(2,1)}, bf16[8,512,256]{2,1,0:T(8,128)(2,1)S(1)}, u32[]{:S(2)}) copy-start(bf16[8,512,256]{2,1,0:T(8,128)(2,1)S(1)} %collective-permute-done.7.refs_9_) | copy-start | bytes 6291460
  110.6 22.9 %collective-permute-start.11 = (bf16[8,128,512]{2,1,0:T(8,128)(2,1)S(1)}, bf16[8,128,512]{2,1,0:T(8,128)(2,1)}, u32[]{:S(2)}, u32[]{:S(2)}) collective-permute-start(bf16[8,128,512]{2,1,0:T(8,128)(2,1)S(1)} %all-to-all-done.1.refs_0_), channel_id=1, source_target_pairs={{0,192},{8,72},{64,0},{72,136},{128,64},{136,200},{192,128},{200,8... | collective-permute-start | bytes 3145736 | tf_op jit(solution)/shard_map/ppermute | solution.py:251
  112.1 25.9 %collective-permute-start.13 = (bf16[8,128,512]{2,1,0:T(8,128)(2,1)}, bf16[8,128,512]{2,1,0:T(8,128)(2,1)}, u32[]{:S(2)}, u32[]{:S(2)}) collective-permute-start(bf16[8,128,512]{2,1,0:T(8,128)(2,1)} %collective-permute-done.8.refs_2_), channel_id=1, source_target_pairs={{0,64},{8,200},{64,128},{72,8},{128,192},{136,72},{192,0},{200,136... | collective-permute-start | bytes 3145736 | tf_op jit(solution)/shard_map/ppermute | solution.py:251
  113.2 34.1 %collective-permute-start.16 = (bf16[8,512,256]{2,1,0:T(8,128)(2,1)S(1)}, bf16[8,512,256]{2,1,0:T(8,128)(2,1)}, u32[]{:S(2)}, u32[]{:S(2)}) collective-permute-start(bf16[8,512,256]{2,1,0:T(8,128)(2,1)S(1)} %collective-permute-done.7.refs_9_), channel_id=1, source_target_pairs={{0,16},{8,56},{16,32},{24,8},{32,48},{40,24},{48,0},{56,40},{1,17}... | collective-permute-start | bytes 6291464 | tf_op jit(solution)/shard_map/ppermute | solution.py:251
  116.3 23.3 %collective-permute-start.9 = (bf16[8,128,512]{2,1,0:T(8,128)(2,1)S(1)}, bf16[8,128,512]{2,1,0:T(8,128)(2,1)}, u32[]{:S(2)}, u32[]{:S(2)}) collective-permute-start(bf16[8,128,512]{2,1,0:T(8,128)(2,1)S(1)} %all-to-all-done.1.refs_0_), channel_id=1, source_target_pairs={{0,8},{8,0},{1,9},{9,1},{2,10},{10,2},{3,11},{11,3},{4,12},{12,4},... | collective-permute-start | bytes 3145736 | tf_op jit(solution)/shard_map/ppermute | solution.py:280
  129.5 10.1 %collective-permute-start.10 = (bf16[8,128,512]{2,1,0:T(8,128)(2,1)}, bf16[8,128,512]{2,1,0:T(8,128)(2,1)}, u32[]{:S(2)}, u32[]{:S(2)}) collective-permute-start(bf16[8,128,512]{2,1,0:T(8,128)(2,1)} %collective-permute-done.8.refs_2_), channel_id=1, source_target_pairs={{0,8},{8,0},{1,9},{9,1},{2,10},{10,2},{3,11},{11,3},{4,12},{12,4},... | collective-permute-start | bytes 3145736 | tf_op jit(solution)/shard_map/ppermute | solution.py:280
  133.5 7.1 %collective-permute-start.12 = (bf16[8,128,512]{2,1,0:T(8,128)(2,1)}, bf16[8,128,512]{2,1,0:T(8,128)(2,1)}, u32[]{:S(2)}, u32[]{:S(2)}) collective-permute-start(bf16[8,128,512]{2,1,0:T(8,128)(2,1)} %collective-permute-done.11.refs_4_), channel_id=1, source_target_pairs={{0,8},{8,0},{1,9},{9,1},{2,10},{10,2},{3,11},{11,3},{4,12},{12,4},... | collective-permute-start | bytes 3145736 | tf_op jit(solution)/shard_map/ppermute | solution.py:280
  138.0 4.1 %collective-permute-start.14 = (bf16[8,128,512]{2,1,0:T(8,128)(2,1)}, bf16[8,128,512]{2,1,0:T(8,128)(2,1)}, u32[]{:S(2)}, u32[]{:S(2)}) collective-permute-start(bf16[8,128,512]{2,1,0:T(8,128)(2,1)} %collective-permute-done.13.refs_6_), channel_id=1, source_target_pairs={{0,8},{8,0},{1,9},{9,1},{2,10},{10,2},{3,11},{11,3},{4,12},{12,4},... | collective-permute-start | bytes 3145736 | tf_op jit(solution)/shard_map/ppermute | solution.py:280
  (8 other events, 133.4 us)

commit v4 on v3

--- a/solution.py
+++ b/solution.py
@@ -65,6 +65,10 @@
                 runs.append(sides.swapaxes(0, 1).reshape(BLOCK // PIECE, 8, HEAD))
             o_ref[:, :, cols] = jnp.concatenate(runs, axis=1).astype(jnp.bfloat16)
 
+    @pl.when(first < 0)
+    def _():
+        o_ref[...] = jnp.zeros_like(o_ref)
+
     @pl.when(first >= 0)
     def _():
         tiles = jnp.int32(1)
@@ -270,7 +274,9 @@
     )
     block_of = block_of.reshape(groups, BAL).T.reshape(-1)
     row_of = (block_of[:, None] * PIECE + jnp.arange(PIECE)[None, :]).reshape(-1)
-    live = jnp.take(arrived.reshape(groups * blocks * PIECE, cols), row_of, axis=0, mode="clip")
+    pick = (row_of[:, None] == jnp.arange(groups * blocks * PIECE)[None, :]).astype(jnp.bfloat16)
+    live = jnp.dot(pick, arrived.reshape(groups * blocks * PIECE, cols), preferred_element_type=jnp.float32)
+    live = live.astype(jnp.bfloat16)
     mine = lax.all_to_all(live.reshape(n_z, groups * PIECE, cols), "z", 0, 0, tiled=True)
     ahead = hop(mine, "y", 1)
     w_ahead, ahead, mine = lax.optimization_barrier((w_ahead, ahead, mine))

time: 203 us -> 200 us (0.985)
  local copies, waits for them, and re-layouts: 6.13 us -> 1.05 us
  matrix products: 0 us -> 3.36 us
    gather x1 -> x0, local copies, waits for them, and re-layouts: 5.07 us -> none  [on_device(): jnp.take(arrived.reshape(groups * blocks * PIECE, cols), row_of, axis=0,...]
    dot_general x0 -> x1, matrix products: none -> 3.36 us  [on_device(): jnp.dot(pick, arrived.reshape(groups * blocks * PIECE, cols), preferred_e...]
where the time goes in v4:
time: 200 us
  waiting for transfers between devices  76 us (38%)
  starting transfers between devices  50 us (25%)
  blocking collectives  35 us (18%)
  Pallas kernels  33.4 us (17%)
  matrix products  3.36 us (2%)
    all_to_all x1, blocking collectives, on_device(): return arrange(lax.all_to_all(projected, PLANE, 0, 0, tiled=True))  35 us
    ppermute x6, waiting for transfers between devices, hop(): return lax.ppermute(mine, (axis, 'c'), pairs)  29.1 us
    all_to_all x1, waiting for transfers between devices, on_device(): lax.all_to_all(live.reshape(n_z, groups * PIECE, cols), 'z', 0, 0, tiled=...  22.6 us
    ppermute x3, waiting for transfers between devices, ring(): before.append(lax.ppermute(before[-1], axis, neighbours(axis, n, 1)))  17.8 us
    pallas_call x1, Pallas kernels, project(): pl.pallas_call(project_kernel, out_shape=jax.ShapeDtypeStruct((groups, 8...  16.7 us
    ppermute x6, starting transfers between devices, hop(): return lax.ppermute(mine, (axis, 'c'), pairs)  11.8 us
    all_to_all x1, starting transfers between devices, on_device(): arrived = lax.all_to_all(pieces, PLANE, 0, 0, tiled=True)  11.5 us
    pallas_call x1, Pallas kernels, attention(): pl.pallas_call(attention_kernel, out_shape=jax.ShapeDtypeStruct((groups,...  10.4 us
  transfers between devices with their start and end apart: 19, of which 10 were waited for; matrix products, arithmetic and copies ran while one was open for 1% of the time, Pallas kernels for 6%

profile of v4, /device:TPU:1, one launch (start us, length us, event | category | flops | bytes accessed | tf_op | source)
XLA Modules:
  0.0 199.8 jit_solution(5134993130817498281)
XLA Ops:
  0.0 2.5 %collective-permute-start = (bf16[512,256]{1,0:T(8,128)(2,1)}, bf16[512,256]{1,0:T(8,128)(2,1)S(1)}, u32[]{:S(2)}, u32[]{:S(2)}) collective-permute-start(bf16[512,256]{1,0:T(8,128)(2,1)} %refs_0_), channel_id=1, source_target_pairs={{0,1},{1,2},{2,3},{3,4},{4,5},{5,6},{6,7},{7,0},{8,9},{9,10},{10,1... | collective-permute-start | bytes 786440 | tf_op jit(solution)/shard_map/ppermute | solution.py:264
  2.5 3.9 %collective-permute-start.1 = (bf16[512,256]{1,0:T(8,128)(2,1)}, bf16[512,256]{1,0:T(8,128)(2,1)S(1)}, u32[]{:S(2)}, u32[]{:S(2)}) collective-permute-start(bf16[512,256]{1,0:T(8,128)(2,1)} %refs_0_), channel_id=1, source_target_pairs={{0,7},{1,0},{2,1},{3,2},{4,3},{5,4},{6,5},{7,6},{8,15},{9,8},{10,9... | collective-permute-start | bytes 786440 | tf_op jit(solution)/shard_map/ppermute | solution.py:264
  6.4 10.4 %attention.1 = bf16[32,64,512]{2,1,0:T(8,128)(2,1)} custom-call(s32[2048]{0:T(1024)} %seg_s.1, bf16[2048,512]{1,0:T(8,128)(2,1)} %q_ref.1, bf16[2048,128]{1,0:T(8,128)(2,1)} %k_ref.1, bf16[2048,128]{1,0:T(8,128)(2,1)} %v_ref.1, s32[1,2048]{1,0:T(1,128)} %bitcast.12), custom_call_target="tpu_custom_call" | custom-call | flops 4294967296 | bytes 6291456 | tf_op jit(solution)/shard_map/attention/pallas_call | solution.py:88
  16.9 11.5 %all-to-all-start = ((bf16[32,64,512]{2,1,0:T(8,128)(2,1)}), bf16[32,64,512]{2,1,0:T(8,128)(2,1)S(1)}, u32[]{:S(2)}, u32[]{:S(2)}) async-start(bf16[32,64,512]{2,1,0:T(8,128)(2,1)} %attention.1), calls=%async_computation | async-start | bytes 4194304 | tf_op jit(solution)/shard_map/all_to_all | solution.py:267
  28.7 2.7 %collective-permute-start.5 = (bf16[512,256]{1,0:T(8,128)(2,1)S(1)}, bf16[512,256]{1,0:T(8,128)(2,1)S(1)}, u32[]{:S(2)}, u32[]{:S(2)}) collective-permute-start(bf16[512,256]{1,0:T(8,128)(2,1)S(1)} %collective-permute-done.1.refs_7_), channel_id=1, source_target_pairs={{0,7},{1,0},{2,1},{3,2},{4,3},{5,4},{6,5},{7,6},{8,15},{9,8},{10,9... | collective-permute-start | bytes 786440 | tf_op jit(solution)/shard_map/ppermute | solution.py:248
  31.4 6.2 %collective-permute-done.2.refs_2_ = bf16[512,256]{1,0:T(8,128)(2,1)S(1)} collective-permute-done((bf16[512,256]{1,0:T(8,128)(2,1)S(1)}, bf16[512,256]{1,0:T(8,128)(2,1)S(1)}, u32[]{:S(2)}, u32[]{:S(2)}) %collective-permute-start.2) | collective-permute-done | bytes 262176 | tf_op jit(solution)/shard_map/ppermute | solution.py:246
  37.8 2.7 %collective-permute-start.6 = (bf16[512,256]{1,0:T(8,128)(2,1)S(1)}, bf16[512,256]{1,0:T(8,128)(2,1)S(1)}, u32[]{:S(2)}, u32[]{:S(2)}) collective-permute-start(bf16[512,256]{1,0:T(8,128)(2,1)S(1)} %collective-permute-done.5.refs_6_), channel_id=1, source_target_pairs={{0,7},{1,0},{2,1},{3,2},{4,3},{5,4},{6,5},{7,6},{8,15},{9,8},{10,9... | collective-permute-start | bytes 786440 | tf_op jit(solution)/shard_map/ppermute | solution.py:248
  40.5 5.0 %collective-permute-done.3.refs_3_ = bf16[512,256]{1,0:T(8,128)(2,1)S(1)} collective-permute-done((bf16[512,256]{1,0:T(8,128)(2,1)S(1)}, bf16[512,256]{1,0:T(8,128)(2,1)S(1)}, u32[]{:S(2)}, u32[]{:S(2)}) %collective-permute-start.3) | collective-permute-done | bytes 262176 | tf_op jit(solution)/shard_map/ppermute | solution.py:246
  46.0 6.5 %collective-permute-done.4.refs_4_ = bf16[512,256]{1,0:T(8,128)(2,1)S(1)} collective-permute-done((bf16[512,256]{1,0:T(8,128)(2,1)S(1)}, bf16[512,256]{1,0:T(8,128)(2,1)S(1)}, u32[]{:S(2)}, u32[]{:S(2)}) %collective-permute-start.4) | collective-permute-done | bytes 262176 | tf_op jit(solution)/shard_map/ppermute | solution.py:246
  52.6 3.7 %all-to-all-done = bf16[32,64,512]{2,1,0:T(8,128)(2,1)S(1)} async-done(((bf16[32,64,512]{2,1,0:T(8,128)(2,1)}), bf16[32,64,512]{2,1,0:T(8,128)(2,1)S(1)}, u32[]{:S(2)}, u32[]{:S(2)}) %all-to-all-start) | async-done | bytes 2097184 | tf_op jit(solution)/shard_map/all_to_all | solution.py:267
  56.3 3.4 %fusion.2 = bf16[1024,512]{1,0:T(8,128)(2,1)} fusion(bf16[2048,512]{1,0:T(8,128)(2,1)S(1)} %bitcast.10, s32[1024]{0:T(1024)S(1)} %add.97), kind=kOutput, calls=%fused_computation.4 | convolution fusion | flops 2150105088 | bytes 3149824 | tf_op jit(solution)/shard_map/dot_general | solution.py:278
  59.7 5.3 %all-to-all-start.1 = ((bf16[8,128,512]{2,1,0:T(8,128)(2,1)}), bf16[8,128,512]{2,1,0:T(8,128)(2,1)S(1)}, u32[]{:S(2)}, u32[]{:S(2)}) async-start(bf16[8,128,512]{2,1,0:T(8,128)(2,1)} %bitcast.5), calls=%async_computation.1 | async-start | bytes 2097152 | tf_op jit(solution)/shard_map/all_to_all | solution.py:280
  65.0 2.4 %join.1.refs_8_ = bf16[8,512,256]{2,1,0:T(8,128)(2,1)} custom-call(bf16[512,256]{1,0:T(8,128)(2,1)} %refs_0_, bf16[512,256]{1,0:T(8,128)(2,1)} %copy-done.2, bf16[512,256]{1,0:T(8,128)(2,1)} %copy-done.4, bf16[512,256]{1,0:T(8,128)(2,1)} %copy-done.6, bf16[512,256]{1,0:T(8,128)(2,1)} %copy-done.8, bf16[512,256]{1,0:T(8,128)(2,1)} %copy-done.7, ...), custom_call_target="tpu_custom_call" | custom-call | bytes 4194304 | tf_op jit(solution)/shard_map/join/pallas_call | solution.py:226
  69.6 22.6 %all-to-all-done.1.refs_0_ = bf16[8,128,512]{2,1,0:T(8,128)(2,1)S(1)} async-done(((bf16[8,128,512]{2,1,0:T(8,128)(2,1)}), bf16[8,128,512]{2,1,0:T(8,128)(2,1)S(1)}, u32[]{:S(2)}, u32[]{:S(2)}) %all-to-all-start.1) | async-done | bytes 1048608 | tf_op jit(solution)/shard_map/all_to_all | solution.py:280
  92.2 2.5 %collective-permute-start.8 = (bf16[8,128,512]{2,1,0:T(8,128)(2,1)S(1)}, bf16[8,128,512]{2,1,0:T(8,128)(2,1)}, u32[]{:S(2)}, u32[]{:S(2)}) collective-permute-start(bf16[8,128,512]{2,1,0:T(8,128)(2,1)S(1)} %all-to-all-done.1.refs_0_), channel_id=1, source_target_pairs={{0,64},{8,200},{64,128},{72,8},{128,192},{136,72},{192,0},{200,136... | collective-permute-start | bytes 3145736 | tf_op jit(solution)/shard_map/ppermute | solution.py:255
  96.2 11.3 %collective-permute-done.8.refs_2_ = bf16[8,128,512]{2,1,0:T(8,128)(2,1)} collective-permute-done((bf16[8,128,512]{2,1,0:T(8,128)(2,1)S(1)}, bf16[8,128,512]{2,1,0:T(8,128)(2,1)}, u32[]{:S(2)}, u32[]{:S(2)}) %collective-permute-start.8) | collective-permute-done | bytes 1048608 | tf_op jit(solution)/shard_map/ppermute | solution.py:255
  110.1 3.0 %collective-permute-start.16 = (bf16[8,512,256]{2,1,0:T(8,128)(2,1)S(1)}, bf16[8,512,256]{2,1,0:T(8,128)(2,1)}, u32[]{:S(2)}, u32[]{:S(2)}) collective-permute-start(bf16[8,512,256]{2,1,0:T(8,128)(2,1)S(1)} %collective-permute-done.7.refs_9_), channel_id=1, source_target_pairs={{0,16},{8,56},{16,32},{24,8},{32,48},{40,24},{48,0},{56,40},{1,17}... | collective-permute-start | bytes 6291464 | tf_op jit(solution)/shard_map/ppermute | solution.py:255
  113.8 12.6 %collective-permute-done.15.refs_10_ = bf16[8,512,256]{2,1,0:T(8,128)(2,1)S(1)} collective-permute-done((bf16[8,512,256]{2,1,0:T(8,128)(2,1)}, bf16[8,512,256]{2,1,0:T(8,128)(2,1)S(1)}, u32[]{:S(2)}, u32[]{:S(2)}) %collective-permute-start.15) | collective-permute-done | bytes 2097184 | tf_op jit(solution)/shard_map/ppermute | solution.py:255
  126.4 4.0 %collective-permute-start.10 = (bf16[8,128,512]{2,1,0:T(8,128)(2,1)}, bf16[8,128,512]{2,1,0:T(8,128)(2,1)}, u32[]{:S(2)}, u32[]{:S(2)}) collective-permute-start(bf16[8,128,512]{2,1,0:T(8,128)(2,1)} %collective-permute-done.8.refs_2_), channel_id=1, source_target_pairs={{0,8},{8,0},{1,9},{9,1},{2,10},{10,2},{3,11},{11,3},{4,12},{12,4},... | collective-permute-start | bytes 3145736 | tf_op jit(solution)/shard_map/ppermute | solution.py:286
  130.4 4.5 %collective-permute-start.12 = (bf16[8,128,512]{2,1,0:T(8,128)(2,1)}, bf16[8,128,512]{2,1,0:T(8,128)(2,1)}, u32[]{:S(2)}, u32[]{:S(2)}) collective-permute-start(bf16[8,128,512]{2,1,0:T(8,128)(2,1)} %collective-permute-done.11.refs_4_), channel_id=1, source_target_pairs={{0,8},{8,0},{1,9},{9,1},{2,10},{10,2},{3,11},{11,3},{4,12},{12,4},... | collective-permute-start | bytes 3145736 | tf_op jit(solution)/shard_map/ppermute | solution.py:286
  139.0 5.2 %collective-permute-done.16.refs_11_ = bf16[8,512,256]{2,1,0:T(8,128)(2,1)} collective-permute-done((bf16[8,512,256]{2,1,0:T(8,128)(2,1)S(1)}, bf16[8,512,256]{2,1,0:T(8,128)(2,1)}, u32[]{:S(2)}, u32[]{:S(2)}) %collective-permute-start.16) | collective-permute-done | bytes 2097184 | tf_op jit(solution)/shard_map/ppermute | solution.py:255
  144.2 16.7 %project.1 = bf16[32,32,1024]{2,1,0:T(8,128)(2,1)} custom-call(s32[13]{0:T(128)} %pad_add_fusion.order_s, bf16[8,128,512]{2,1,0:T(8,128)(2,1)} %copy-done.1, bf16[8,128,512]{2,1,0:T(8,128)(2,1)} %collective-permute-done.9.refs_1_, bf16[8,128,512]{2,1,0:T(8,128)(2,1)} %collective-permute-done.8.refs_2_, bf16[8,128,512]{2,1,0:T(8,128)(2,1)} %collective-permute-done.10.refs_3_, ...), custom_call_target="tpu_custom_call" | custom-call | flops 8589934592 | bytes 18874368 | tf_op jit(solution)/shard_map/project/pallas_call | solution.py:159
  161.0 35.0 %all_to_all.15 = bf16[32,32,1024]{2,1,0:T(8,128)(2,1)} all-to-all(bf16[32,32,1024]{2,1,0:T(8,128)(2,1)} %project.1), channel_id=1, replica_groups=mesh['y'=4,'x'=4,'c'=2,'z'=8] {'y','x','c'}, dimensions={0} | all-to-all | bytes 4194304 | tf_op jit(solution)/shard_map/all_to_all | solution.py:294
  196.0 3.8 %arrange.1 = bf16[128,8192]{1,0:T(8,128)(2,1)} custom-call(bf16[4,4,2,32,1024]{4,3,2,1,0:T(8,128)(2,1)} %bitcast.9), custom_call_target="tpu_custom_call" | custom-call | bytes 4194304 | tf_op jit(solution)/shard_map/arrange/pallas_call | solution.py:195
  (58 shorter events, 12.0 us)
Async XLA Ops:
  0.0 16.9 %collective-permute-start = (bf16[512,256]{1,0:T(8,128)(2,1)}, bf16[512,256]{1,0:T(8,128)(2,1)S(1)}, u32[]{:S(2)}, u32[]{:S(2)}) collective-permute-start(bf16[512,256]{1,0:T(8,128)(2,1)} %refs_0_), channel_id=1, source_target_pairs={{0,1},{1,2},{2,3},{3,4},{4,5},{5,6},{6,7},{7,0},{8,9},{9,10},{10,1... | collective-permute-start | bytes 786440 | tf_op jit(solution)/shard_map/ppermute | solution.py:264
  2.5 14.4 %collective-permute-start.1 = (bf16[512,256]{1,0:T(8,128)(2,1)}, bf16[512,256]{1,0:T(8,128)(2,1)S(1)}, u32[]{:S(2)}, u32[]{:S(2)}) collective-permute-start(bf16[512,256]{1,0:T(8,128)(2,1)} %refs_0_), channel_id=1, source_target_pairs={{0,7},{1,0},{2,1},{3,2},{4,3},{5,4},{6,5},{7,6},{8,15},{9,8},{10,9... | collective-permute-start | bytes 786440 | tf_op jit(solution)/shard_map/ppermute | solution.py:264
  16.9 39.4 %all-to-all-start = ((bf16[32,64,512]{2,1,0:T(8,128)(2,1)}), bf16[32,64,512]{2,1,0:T(8,128)(2,1)S(1)}, u32[]{:S(2)}, u32[]{:S(2)}) async-start(bf16[32,64,512]{2,1,0:T(8,128)(2,1)} %attention.1), calls=%async_computation | async-start | bytes 4194304 | tf_op jit(solution)/shard_map/all_to_all | solution.py:267
  28.4 9.1 %collective-permute-start.2 = (bf16[512,256]{1,0:T(8,128)(2,1)S(1)}, bf16[512,256]{1,0:T(8,128)(2,1)S(1)}, u32[]{:S(2)}, u32[]{:S(2)}) collective-permute-start(bf16[512,256]{1,0:T(8,128)(2,1)S(1)} %collective-permute-done.refs_1_), channel_id=1, source_target_pairs={{0,1},{1,2},{2,3},{3,4},{4,5},{5,6},{6,7},{7,0},{8,9},{9,10},{10,1... | collective-permute-start | bytes 786440 | tf_op jit(solution)/shard_map/ppermute | solution.py:246
  28.7 9.0 %collective-permute-start.5 = (bf16[512,256]{1,0:T(8,128)(2,1)S(1)}, bf16[512,256]{1,0:T(8,128)(2,1)S(1)}, u32[]{:S(2)}, u32[]{:S(2)}) collective-permute-start(bf16[512,256]{1,0:T(8,128)(2,1)S(1)} %collective-permute-done.1.refs_7_), channel_id=1, source_target_pairs={{0,7},{1,0},{2,1},{3,2},{4,3},{5,4},{6,5},{7,6},{8,15},{9,8},{10,9... | collective-permute-start | bytes 786440 | tf_op jit(solution)/shard_map/ppermute | solution.py:248
  37.6 22.1 %copy-start.4 = (bf16[512,256]{1,0:T(8,128)(2,1)}, bf16[512,256]{1,0:T(8,128)(2,1)S(1)}, u32[]{:S(2)}) copy-start(bf16[512,256]{1,0:T(8,128)(2,1)S(1)} %collective-permute-done.2.refs_2_) | copy-start | bytes 786436
  37.6 8.0 %collective-permute-start.3 = (bf16[512,256]{1,0:T(8,128)(2,1)S(1)}, bf16[512,256]{1,0:T(8,128)(2,1)S(1)}, u32[]{:S(2)}, u32[]{:S(2)}) collective-permute-start(bf16[512,256]{1,0:T(8,128)(2,1)S(1)} %collective-permute-done.2.refs_2_), channel_id=1, source_target_pairs={{0,1},{1,2},{2,3},{3,4},{4,5},{5,6},{6,7},{7,0},{8,9},{9,10},{10,1... | collective-permute-start | bytes 786440 | tf_op jit(solution)/shard_map/ppermute | solution.py:246
  37.8 8.3 %collective-permute-start.6 = (bf16[512,256]{1,0:T(8,128)(2,1)S(1)}, bf16[512,256]{1,0:T(8,128)(2,1)S(1)}, u32[]{:S(2)}, u32[]{:S(2)}) collective-permute-start(bf16[512,256]{1,0:T(8,128)(2,1)S(1)} %collective-permute-done.5.refs_6_), channel_id=1, source_target_pairs={{0,7},{1,0},{2,1},{3,2},{4,3},{5,4},{6,5},{7,6},{8,15},{9,8},{10,9... | collective-permute-start | bytes 786440 | tf_op jit(solution)/shard_map/ppermute | solution.py:248
  45.5 7.0 %collective-permute-start.4 = (bf16[512,256]{1,0:T(8,128)(2,1)S(1)}, bf16[512,256]{1,0:T(8,128)(2,1)S(1)}, u32[]{:S(2)}, u32[]{:S(2)}) collective-permute-start(bf16[512,256]{1,0:T(8,128)(2,1)S(1)} %collective-permute-done.3.refs_3_), channel_id=1, source_target_pairs={{0,1},{1,2},{2,3},{3,4},{4,5},{5,6},{6,7},{7,0},{8,9},{9,10},{10,1... | collective-permute-start | bytes 786440 | tf_op jit(solution)/shard_map/ppermute | solution.py:246
  59.7 32.5 %all-to-all-start.1 = ((bf16[8,128,512]{2,1,0:T(8,128)(2,1)}), bf16[8,128,512]{2,1,0:T(8,128)(2,1)S(1)}, u32[]{:S(2)}, u32[]{:S(2)}) async-start(bf16[8,128,512]{2,1,0:T(8,128)(2,1)} %bitcast.5), calls=%async_computation.1 | async-start | bytes 2097152 | tf_op jit(solution)/shard_map/all_to_all | solution.py:280
  65.0 70.1 %copy-start = (s32[2,4]{1,0:T(2,128)S(1)}, s32[2,4]{1,0:T(2,128)}, u32[]{:S(2)}) copy-start(s32[2,4]{1,0:T(2,128)} %constant.87.clone) | copy-start | bytes 100
  65.0 70.7 %copy-start.10 = (s32[4]{0:T(128)S(1)}, s32[4]{0:T(128)}, u32[]{:S(2)}) copy-start(s32[4]{0:T(128)} %constant.88.clone) | copy-start | bytes 52
  67.4 28.8 %collective-permute-start.7 = (bf16[8,512,256]{2,1,0:T(8,128)(2,1)}, bf16[8,512,256]{2,1,0:T(8,128)(2,1)S(1)}, u32[]{:S(2)}, u32[]{:S(2)}) collective-permute-start(bf16[8,512,256]{2,1,0:T(8,128)(2,1)} %join.1.refs_8_), channel_id=1, source_target_pairs={{0,16},{8,56},{16,32},{24,8},{32,48},{40,24},{48,0},{56,40},{1,17}... | collective-permute-start | bytes 6291464 | tf_op jit(solution)/shard_map/ppermute | solution.py:255
  92.2 52.0 %copy-start.1 = (bf16[8,128,512]{2,1,0:T(8,128)(2,1)}, bf16[8,128,512]{2,1,0:T(8,128)(2,1)S(1)}, u32[]{:S(2)}) copy-start(bf16[8,128,512]{2,1,0:T(8,128)(2,1)S(1)} %all-to-all-done.1.refs_0_) | copy-start | bytes 3145732
  92.2 15.3 %collective-permute-start.8 = (bf16[8,128,512]{2,1,0:T(8,128)(2,1)S(1)}, bf16[8,128,512]{2,1,0:T(8,128)(2,1)}, u32[]{:S(2)}, u32[]{:S(2)}) collective-permute-start(bf16[8,128,512]{2,1,0:T(8,128)(2,1)S(1)} %all-to-all-done.1.refs_0_), channel_id=1, source_target_pairs={{0,64},{8,200},{64,128},{72,8},{128,192},{136,72},{192,0},{200,136... | collective-permute-start | bytes 3145736 | tf_op jit(solution)/shard_map/ppermute | solution.py:255
  94.6 31.8 %collective-permute-start.15 = (bf16[8,512,256]{2,1,0:T(8,128)(2,1)}, bf16[8,512,256]{2,1,0:T(8,128)(2,1)S(1)}, u32[]{:S(2)}, u32[]{:S(2)}) collective-permute-start(bf16[8,512,256]{2,1,0:T(8,128)(2,1)} %join.1.refs_8_), channel_id=1, source_target_pairs={{0,48},{8,24},{16,0},{24,40},{32,16},{40,56},{48,32},{56,8},{1,49}... | collective-permute-start | bytes 6291464 | tf_op jit(solution)/shard_map/ppermute | solution.py:255
  96.1 48.1 %copy-start.11 = (bf16[8,512,256]{2,1,0:T(8,128)(2,1)}, bf16[8,512,256]{2,1,0:T(8,128)(2,1)S(1)}, u32[]{:S(2)}) copy-start(bf16[8,512,256]{2,1,0:T(8,128)(2,1)S(1)} %collective-permute-done.7.refs_9_) | copy-start | bytes 6291460
  107.5 22.9 %collective-permute-start.11 = (bf16[8,128,512]{2,1,0:T(8,128)(2,1)S(1)}, bf16[8,128,512]{2,1,0:T(8,128)(2,1)}, u32[]{:S(2)}, u32[]{:S(2)}) collective-permute-start(bf16[8,128,512]{2,1,0:T(8,128)(2,1)S(1)} %all-to-all-done.1.refs_0_), channel_id=1, source_target_pairs={{0,192},{8,72},{64,0},{72,136},{128,64},{136,200},{192,128},{200,8... | collective-permute-start | bytes 3145736 | tf_op jit(solution)/shard_map/ppermute | solution.py:255
  109.0 25.9 %collective-permute-start.13 = (bf16[8,128,512]{2,1,0:T(8,128)(2,1)}, bf16[8,128,512]{2,1,0:T(8,128)(2,1)}, u32[]{:S(2)}, u32[]{:S(2)}) collective-permute-start(bf16[8,128,512]{2,1,0:T(8,128)(2,1)} %collective-permute-done.8.refs_2_), channel_id=1, source_target_pairs={{0,64},{8,200},{64,128},{72,8},{128,192},{136,72},{192,0},{200,136... | collective-permute-start | bytes 3145736 | tf_op jit(solution)/shard_map/ppermute | solution.py:255
  110.1 34.1 %collective-permute-start.16 = (bf16[8,512,256]{2,1,0:T(8,128)(2,1)S(1)}, bf16[8,512,256]{2,1,0:T(8,128)(2,1)}, u32[]{:S(2)}, u32[]{:S(2)}) collective-permute-start(bf16[8,512,256]{2,1,0:T(8,128)(2,1)S(1)} %collective-permute-done.7.refs_9_), channel_id=1, source_target_pairs={{0,16},{8,56},{16,32},{24,8},{32,48},{40,24},{48,0},{56,40},{1,17}... | collective-permute-start | bytes 6291464 | tf_op jit(solution)/shard_map/ppermute | solution.py:255
  113.2 23.1 %collective-permute-start.9 = (bf16[8,128,512]{2,1,0:T(8,128)(2,1)S(1)}, bf16[8,128,512]{2,1,0:T(8,128)(2,1)}, u32[]{:S(2)}, u32[]{:S(2)}) collective-permute-start(bf16[8,128,512]{2,1,0:T(8,128)(2,1)S(1)} %all-to-all-done.1.refs_0_), channel_id=1, source_target_pairs={{0,8},{8,0},{1,9},{9,1},{2,10},{10,2},{3,11},{11,3},{4,12},{12,4},... | collective-permute-start | bytes 3145736 | tf_op jit(solution)/shard_map/ppermute | solution.py:286
  126.4 9.9 %collective-permute-start.10 = (bf16[8,128,512]{2,1,0:T(8,128)(2,1)}, bf16[8,128,512]{2,1,0:T(8,128)(2,1)}, u32[]{:S(2)}, u32[]{:S(2)}) collective-permute-start(bf16[8,128,512]{2,1,0:T(8,128)(2,1)} %collective-permute-done.8.refs_2_), channel_id=1, source_target_pairs={{0,8},{8,0},{1,9},{9,1},{2,10},{10,2},{3,11},{11,3},{4,12},{12,4},... | collective-permute-start | bytes 3145736 | tf_op jit(solution)/shard_map/ppermute | solution.py:286
  130.4 7.1 %collective-permute-start.12 = (bf16[8,128,512]{2,1,0:T(8,128)(2,1)}, bf16[8,128,512]{2,1,0:T(8,128)(2,1)}, u32[]{:S(2)}, u32[]{:S(2)}) collective-permute-start(bf16[8,128,512]{2,1,0:T(8,128)(2,1)} %collective-permute-done.11.refs_4_), channel_id=1, source_target_pairs={{0,8},{8,0},{1,9},{9,1},{2,10},{10,2},{3,11},{11,3},{4,12},{12,4},... | collective-permute-start | bytes 3145736 | tf_op jit(solution)/shard_map/ppermute | solution.py:286
  134.9 4.1 %collective-permute-start.14 = (bf16[8,128,512]{2,1,0:T(8,128)(2,1)}, bf16[8,128,512]{2,1,0:T(8,128)(2,1)}, u32[]{:S(2)}, u32[]{:S(2)}) collective-permute-start(bf16[8,128,512]{2,1,0:T(8,128)(2,1)} %collective-permute-done.13.refs_6_), channel_id=1, source_target_pairs={{0,8},{8,0},{1,9},{9,1},{2,10},{10,2},{3,11},{11,3},{4,12},{12,4},... | collective-permute-start | bytes 3145736 | tf_op jit(solution)/shard_map/ppermute | solution.py:286
  (8 other events, 123.1 us)

commit v5 on v3

--- a/solution.py
+++ b/solution.py
@@ -191,9 +191,9 @@
     return pl.pallas_call(
         arrange_kernel,
         out_shape=jax.ShapeDtypeStruct((n_x * rows, n_y * n_c * cols), jnp.bfloat16),
-        grid=(n_x,),
-        in_specs=[pl.BlockSpec((n_y, 1, n_c, rows, cols), lambda x: (0, x, 0, 0, 0))],
-        out_specs=pl.BlockSpec((rows, n_y * n_c * cols), lambda x: (x, 0)),
+        grid=(n_x, 2),
+        in_specs=[pl.BlockSpec((n_y // 2, 1, n_c, rows, cols), lambda x, half: (half, x, 0, 0, 0))],
+        out_specs=pl.BlockSpec((rows, n_y * n_c * cols // 2), lambda x, half: (x, half)),
         compiler_params=pltpu.CompilerParams(vmem_limit_bytes=56 * MB),
         cost_estimate=pl.CostEstimate(flops=0, bytes_accessed=4 * MB, transcendentals=0),
         name="arrange",

time: 203 us -> 205 us (level)
  Pallas kernels: 33.3 us -> 39.8 us
  starting transfers between devices: 51.6 us -> 46.7 us
    all_to_all x1, starting transfers between devices: 12.7 us -> 7.78 us  [on_device(): arrived = lax.all_to_all(pieces, PLANE, 0, 0, tiled=True)]
    pallas_call x1, Pallas kernels: 10.4 us -> 15 us  [attention(): pl.pallas_call(attention_kernel, out_shape=jax.ShapeDtypeStruct((groups,...]
  transfers between devices with their start and end apart: 19 -> 19, of which waited for: 10 -> 10; matrix products, arithmetic and copies ran while one was open for 1% -> 1% of each run, Pallas kernels for 6% -> 9%
where the time goes in v5:
time: 205 us; the launch traced here: 204 us
  waiting for transfers between devices  75.8 us (37%)
  starting transfers between devices  46.7 us (23%)
  Pallas kernels  39.8 us (19%)
  blocking collectives  35 us (17%)
  local copies, waits for them, and re-layouts  6.13 us (3%)
    all_to_all x1, blocking collectives, on_device(): return arrange(lax.all_to_all(projected, PLANE, 0, 0, tiled=True))  35 us
    ppermute x6, waiting for transfers between devices, hop(): return lax.ppermute(mine, (axis, 'c'), pairs)  29.1 us
    all_to_all x1, waiting for transfers between devices, on_device(): lax.all_to_all(live.reshape(n_z, groups * PIECE, cols), 'z', 0, 0, tiled=...  22.6 us
    ppermute x3, waiting for transfers between devices, ring(): before.append(lax.ppermute(before[-1], axis, neighbours(axis, n, 1)))  17.8 us
    pallas_call x1, Pallas kernels, project(): pl.pallas_call(project_kernel, out_shape=jax.ShapeDtypeStruct((groups, 8...  16.7 us
    pallas_call x1, Pallas kernels, attention(): pl.pallas_call(attention_kernel, out_shape=jax.ShapeDtypeStruct((groups,...  15 us
    ppermute x6, starting transfers between devices, hop(): return lax.ppermute(mine, (axis, 'c'), pairs)  11.8 us
    ppermute x4, starting transfers between devices, on_device(): parts += [part, lax.ppermute(part, 'c', [(0, 1), (1, 0)])]  9.41 us
  transfers between devices with their start and end apart: 19, of which 10 were waited for; matrix products, arithmetic and copies ran while one was open for 1% of the time, Pallas kernels for 9%

profile of v5, /device:TPU:1, one launch (start us, length us, event | category | flops | bytes accessed | tf_op | source)
XLA Modules:
  0.0 204.5 jit_solution(1548902503534971921)
XLA Ops:
  0.0 2.5 %collective-permute-start = (bf16[512,256]{1,0:T(8,128)(2,1)}, bf16[512,256]{1,0:T(8,128)(2,1)S(1)}, u32[]{:S(2)}, u32[]{:S(2)}) collective-permute-start(bf16[512,256]{1,0:T(8,128)(2,1)} %refs_0_), channel_id=1, source_target_pairs={{0,1},{1,2},{2,3},{3,4},{4,5},{5,6},{6,7},{7,0},{8,9},{9,10},{10,1... | collective-permute-start | bytes 786440 | tf_op jit(solution)/shard_map/ppermute | solution.py:260
  2.5 3.9 %collective-permute-start.1 = (bf16[512,256]{1,0:T(8,128)(2,1)}, bf16[512,256]{1,0:T(8,128)(2,1)S(1)}, u32[]{:S(2)}, u32[]{:S(2)}) collective-permute-start(bf16[512,256]{1,0:T(8,128)(2,1)} %refs_0_), channel_id=1, source_target_pairs={{0,7},{1,0},{2,1},{3,2},{4,3},{5,4},{6,5},{7,6},{8,15},{9,8},{10,9... | collective-permute-start | bytes 786440 | tf_op jit(solution)/shard_map/ppermute | solution.py:260
  6.4 15.0 %attention.1 = bf16[32,64,512]{2,1,0:T(8,128)(2,1)} custom-call(s32[2048]{0:T(1024)} %seg_s.1, bf16[2048,512]{1,0:T(8,128)(2,1)} %q_ref.1, bf16[2048,128]{1,0:T(8,128)(2,1)} %k_ref.1, bf16[2048,128]{1,0:T(8,128)(2,1)} %v_ref.1, s32[1,2048]{1,0:T(1,128)} %bitcast.11), custom_call_target="tpu_custom_call" | custom-call | flops 4294967296 | bytes 6291456 | tf_op jit(solution)/shard_map/attention/pallas_call | solution.py:84
  21.5 7.8 %all-to-all-start = ((bf16[32,64,512]{2,1,0:T(8,128)(2,1)}), bf16[32,64,512]{2,1,0:T(8,128)(2,1)S(1)}, u32[]{:S(2)}, u32[]{:S(2)}) async-start(bf16[32,64,512]{2,1,0:T(8,128)(2,1)} %attention.1), calls=%async_computation | async-start | bytes 4194304 | tf_op jit(solution)/shard_map/all_to_all | solution.py:263
  29.5 2.7 %collective-permute-start.5 = (bf16[512,256]{1,0:T(8,128)(2,1)S(1)}, bf16[512,256]{1,0:T(8,128)(2,1)S(1)}, u32[]{:S(2)}, u32[]{:S(2)}) collective-permute-start(bf16[512,256]{1,0:T(8,128)(2,1)S(1)} %collective-permute-done.1.refs_7_), channel_id=1, source_target_pairs={{0,7},{1,0},{2,1},{3,2},{4,3},{5,4},{6,5},{7,6},{8,15},{9,8},{10,9... | collective-permute-start | bytes 786440 | tf_op jit(solution)/shard_map/ppermute | solution.py:244
  32.2 6.2 %collective-permute-done.2.refs_2_ = bf16[512,256]{1,0:T(8,128)(2,1)S(1)} collective-permute-done((bf16[512,256]{1,0:T(8,128)(2,1)S(1)}, bf16[512,256]{1,0:T(8,128)(2,1)S(1)}, u32[]{:S(2)}, u32[]{:S(2)}) %collective-permute-start.2) | collective-permute-done | bytes 262176 | tf_op jit(solution)/shard_map/ppermute | solution.py:242
  38.8 2.7 %collective-permute-start.6 = (bf16[512,256]{1,0:T(8,128)(2,1)S(1)}, bf16[512,256]{1,0:T(8,128)(2,1)S(1)}, u32[]{:S(2)}, u32[]{:S(2)}) collective-permute-start(bf16[512,256]{1,0:T(8,128)(2,1)S(1)} %collective-permute-done.5.refs_6_), channel_id=1, source_target_pairs={{0,7},{1,0},{2,1},{3,2},{4,3},{5,4},{6,5},{7,6},{8,15},{9,8},{10,9... | collective-permute-start | bytes 786440 | tf_op jit(solution)/shard_map/ppermute | solution.py:244
  41.5 4.8 %collective-permute-done.3.refs_3_ = bf16[512,256]{1,0:T(8,128)(2,1)S(1)} collective-permute-done((bf16[512,256]{1,0:T(8,128)(2,1)S(1)}, bf16[512,256]{1,0:T(8,128)(2,1)S(1)}, u32[]{:S(2)}, u32[]{:S(2)}) %collective-permute-start.3) | collective-permute-done | bytes 262176 | tf_op jit(solution)/shard_map/ppermute | solution.py:242
  46.6 6.8 %collective-permute-done.4.refs_4_ = bf16[512,256]{1,0:T(8,128)(2,1)S(1)} collective-permute-done((bf16[512,256]{1,0:T(8,128)(2,1)S(1)}, bf16[512,256]{1,0:T(8,128)(2,1)S(1)}, u32[]{:S(2)}, u32[]{:S(2)}) %collective-permute-start.4) | collective-permute-done | bytes 262176 | tf_op jit(solution)/shard_map/ppermute | solution.py:242
  53.4 3.7 %all-to-all-done = bf16[32,64,512]{2,1,0:T(8,128)(2,1)S(1)} async-done(((bf16[32,64,512]{2,1,0:T(8,128)(2,1)}), bf16[32,64,512]{2,1,0:T(8,128)(2,1)S(1)}, u32[]{:S(2)}, u32[]{:S(2)}) %all-to-all-start) | async-done | bytes 2097184 | tf_op jit(solution)/shard_map/all_to_all | solution.py:263
  57.1 5.1 %gather_fusion.1 = bf16[1024,512]{1,0:T(8,128)(2,1)} fusion(bf16[2048,512]{1,0:T(8,128)(2,1)S(1)} %bitcast.8, s32[1024]{0:T(1024)S(1)} %broadcast_clamp_fusion), kind=kCustom, calls=%fused_computation.1 | custom fusion | bytes 2101248 | tf_op jit(solution)/shard_map/jit(_take)/gather | solution.py:273
  62.2 5.6 %all-to-all-start.1 = ((bf16[8,128,512]{2,1,0:T(8,128)(2,1)}), bf16[8,128,512]{2,1,0:T(8,128)(2,1)S(1)}, u32[]{:S(2)}, u32[]{:S(2)}) async-start(bf16[8,128,512]{2,1,0:T(8,128)(2,1)} %bitcast.5), calls=%async_computation.1 | async-start | bytes 2097152 | tf_op jit(solution)/shard_map/all_to_all | solution.py:274
  67.8 2.4 %join.1.refs_8_ = bf16[8,512,256]{2,1,0:T(8,128)(2,1)} custom-call(bf16[512,256]{1,0:T(8,128)(2,1)} %refs_0_, bf16[512,256]{1,0:T(8,128)(2,1)} %copy-done.2, bf16[512,256]{1,0:T(8,128)(2,1)} %copy-done.4, bf16[512,256]{1,0:T(8,128)(2,1)} %copy-done.6, bf16[512,256]{1,0:T(8,128)(2,1)} %copy-done.8, bf16[512,256]{1,0:T(8,128)(2,1)} %copy-done.7, ...), custom_call_target="tpu_custom_call" | custom-call | bytes 4194304 | tf_op jit(solution)/shard_map/join/pallas_call | solution.py:222
  72.4 22.6 %all-to-all-done.1.refs_0_ = bf16[8,128,512]{2,1,0:T(8,128)(2,1)S(1)} async-done(((bf16[8,128,512]{2,1,0:T(8,128)(2,1)}), bf16[8,128,512]{2,1,0:T(8,128)(2,1)S(1)}, u32[]{:S(2)}, u32[]{:S(2)}) %all-to-all-start.1) | async-done | bytes 1048608 | tf_op jit(solution)/shard_map/all_to_all | solution.py:274
  95.0 2.5 %collective-permute-start.8 = (bf16[8,128,512]{2,1,0:T(8,128)(2,1)S(1)}, bf16[8,128,512]{2,1,0:T(8,128)(2,1)}, u32[]{:S(2)}, u32[]{:S(2)}) collective-permute-start(bf16[8,128,512]{2,1,0:T(8,128)(2,1)S(1)} %all-to-all-done.1.refs_0_), channel_id=1, source_target_pairs={{0,64},{8,200},{64,128},{72,8},{128,192},{136,72},{192,0},{200,136... | collective-permute-start | bytes 3145736 | tf_op jit(solution)/shard_map/ppermute | solution.py:251
  99.0 11.3 %collective-permute-done.8.refs_2_ = bf16[8,128,512]{2,1,0:T(8,128)(2,1)} collective-permute-done((bf16[8,128,512]{2,1,0:T(8,128)(2,1)S(1)}, bf16[8,128,512]{2,1,0:T(8,128)(2,1)}, u32[]{:S(2)}, u32[]{:S(2)}) %collective-permute-start.8) | collective-permute-done | bytes 1048608 | tf_op jit(solution)/shard_map/ppermute | solution.py:251
  113.0 3.0 %collective-permute-start.16 = (bf16[8,512,256]{2,1,0:T(8,128)(2,1)S(1)}, bf16[8,512,256]{2,1,0:T(8,128)(2,1)}, u32[]{:S(2)}, u32[]{:S(2)}) collective-permute-start(bf16[8,512,256]{2,1,0:T(8,128)(2,1)S(1)} %collective-permute-done.7.refs_9_), channel_id=1, source_target_pairs={{0,16},{8,56},{16,32},{24,8},{32,48},{40,24},{48,0},{56,40},{1,17}... | collective-permute-start | bytes 6291464 | tf_op jit(solution)/shard_map/ppermute | solution.py:251
  116.6 12.6 %collective-permute-done.15.refs_10_ = bf16[8,512,256]{2,1,0:T(8,128)(2,1)S(1)} collective-permute-done((bf16[8,512,256]{2,1,0:T(8,128)(2,1)}, bf16[8,512,256]{2,1,0:T(8,128)(2,1)S(1)}, u32[]{:S(2)}, u32[]{:S(2)}) %collective-permute-start.15) | collective-permute-done | bytes 2097184 | tf_op jit(solution)/shard_map/ppermute | solution.py:251
  129.2 4.0 %collective-permute-start.10 = (bf16[8,128,512]{2,1,0:T(8,128)(2,1)}, bf16[8,128,512]{2,1,0:T(8,128)(2,1)}, u32[]{:S(2)}, u32[]{:S(2)}) collective-permute-start(bf16[8,128,512]{2,1,0:T(8,128)(2,1)} %collective-permute-done.8.refs_2_), channel_id=1, source_target_pairs={{0,8},{8,0},{1,9},{9,1},{2,10},{10,2},{3,11},{11,3},{4,12},{12,4},... | collective-permute-start | bytes 3145736 | tf_op jit(solution)/shard_map/ppermute | solution.py:280
  133.2 4.5 %collective-permute-start.12 = (bf16[8,128,512]{2,1,0:T(8,128)(2,1)}, bf16[8,128,512]{2,1,0:T(8,128)(2,1)}, u32[]{:S(2)}, u32[]{:S(2)}) collective-permute-start(bf16[8,128,512]{2,1,0:T(8,128)(2,1)} %collective-permute-done.11.refs_4_), channel_id=1, source_target_pairs={{0,8},{8,0},{1,9},{9,1},{2,10},{10,2},{3,11},{11,3},{4,12},{12,4},... | collective-permute-start | bytes 3145736 | tf_op jit(solution)/shard_map/ppermute | solution.py:280
  141.8 5.2 %collective-permute-done.16.refs_11_ = bf16[8,512,256]{2,1,0:T(8,128)(2,1)} collective-permute-done((bf16[8,512,256]{2,1,0:T(8,128)(2,1)S(1)}, bf16[8,512,256]{2,1,0:T(8,128)(2,1)}, u32[]{:S(2)}, u32[]{:S(2)}) %collective-permute-start.16) | collective-permute-done | bytes 2097184 | tf_op jit(solution)/shard_map/ppermute | solution.py:251
  147.1 16.7 %project.1 = bf16[32,32,1024]{2,1,0:T(8,128)(2,1)} custom-call(s32[13]{0:T(128)} %pad_add_fusion.order_s, bf16[8,128,512]{2,1,0:T(8,128)(2,1)} %copy-done.1, bf16[8,128,512]{2,1,0:T(8,128)(2,1)} %collective-permute-done.9.refs_1_, bf16[8,128,512]{2,1,0:T(8,128)(2,1)} %collective-permute-done.8.refs_2_, bf16[8,128,512]{2,1,0:T(8,128)(2,1)} %collective-permute-done.10.refs_3_, ...), custom_call_target="tpu_custom_call" | custom-call | flops 8589934592 | bytes 18874368 | tf_op jit(solution)/shard_map/project/pallas_call | solution.py:155
  163.8 35.0 %all_to_all.15 = bf16[32,32,1024]{2,1,0:T(8,128)(2,1)} all-to-all(bf16[32,32,1024]{2,1,0:T(8,128)(2,1)} %project.1), channel_id=1, replica_groups=mesh['y'=4,'x'=4,'c'=2,'z'=8] {'y','x','c'}, dimensions={0} | all-to-all | bytes 4194304 | tf_op jit(solution)/shard_map/all_to_all | solution.py:288
  198.8 5.6 %arrange.1 = bf16[128,8192]{1,0:T(8,128)(2,1)} custom-call(bf16[4,4,2,32,1024]{4,3,2,1,0:T(8,128)(2,1)} %bitcast.9), custom_call_target="tpu_custom_call" | custom-call | bytes 4194304 | tf_op jit(solution)/shard_map/arrange/pallas_call | solution.py:191
  (59 shorter events, 12.0 us)
Async XLA Ops:
  0.0 21.4 %collective-permute-start = (bf16[512,256]{1,0:T(8,128)(2,1)}, bf16[512,256]{1,0:T(8,128)(2,1)S(1)}, u32[]{:S(2)}, u32[]{:S(2)}) collective-permute-start(bf16[512,256]{1,0:T(8,128)(2,1)} %refs_0_), channel_id=1, source_target_pairs={{0,1},{1,2},{2,3},{3,4},{4,5},{5,6},{6,7},{7,0},{8,9},{9,10},{10,1... | collective-permute-start | bytes 786440 | tf_op jit(solution)/shard_map/ppermute | solution.py:260
  2.5 19.0 %collective-permute-start.1 = (bf16[512,256]{1,0:T(8,128)(2,1)}, bf16[512,256]{1,0:T(8,128)(2,1)S(1)}, u32[]{:S(2)}, u32[]{:S(2)}) collective-permute-start(bf16[512,256]{1,0:T(8,128)(2,1)} %refs_0_), channel_id=1, source_target_pairs={{0,7},{1,0},{2,1},{3,2},{4,3},{5,4},{6,5},{7,6},{8,15},{9,8},{10,9... | collective-permute-start | bytes 786440 | tf_op jit(solution)/shard_map/ppermute | solution.py:260
  21.5 35.6 %all-to-all-start = ((bf16[32,64,512]{2,1,0:T(8,128)(2,1)}), bf16[32,64,512]{2,1,0:T(8,128)(2,1)S(1)}, u32[]{:S(2)}, u32[]{:S(2)}) async-start(bf16[32,64,512]{2,1,0:T(8,128)(2,1)} %attention.1), calls=%async_computation | async-start | bytes 4194304 | tf_op jit(solution)/shard_map/all_to_all | solution.py:263
  29.3 9.1 %collective-permute-start.2 = (bf16[512,256]{1,0:T(8,128)(2,1)S(1)}, bf16[512,256]{1,0:T(8,128)(2,1)S(1)}, u32[]{:S(2)}, u32[]{:S(2)}) collective-permute-start(bf16[512,256]{1,0:T(8,128)(2,1)S(1)} %collective-permute-done.refs_1_), channel_id=1, source_target_pairs={{0,1},{1,2},{2,3},{3,4},{4,5},{5,6},{6,7},{7,0},{8,9},{9,10},{10,1... | collective-permute-start | bytes 786440 | tf_op jit(solution)/shard_map/ppermute | solution.py:242
  29.5 9.3 %collective-permute-start.5 = (bf16[512,256]{1,0:T(8,128)(2,1)S(1)}, bf16[512,256]{1,0:T(8,128)(2,1)S(1)}, u32[]{:S(2)}, u32[]{:S(2)}) collective-permute-start(bf16[512,256]{1,0:T(8,128)(2,1)S(1)} %collective-permute-done.1.refs_7_), channel_id=1, source_target_pairs={{0,7},{1,0},{2,1},{3,2},{4,3},{5,4},{6,5},{7,6},{8,15},{9,8},{10,9... | collective-permute-start | bytes 786440 | tf_op jit(solution)/shard_map/ppermute | solution.py:244
  38.4 23.8 %copy-start.4 = (bf16[512,256]{1,0:T(8,128)(2,1)}, bf16[512,256]{1,0:T(8,128)(2,1)S(1)}, u32[]{:S(2)}) copy-start(bf16[512,256]{1,0:T(8,128)(2,1)S(1)} %collective-permute-done.2.refs_2_) | copy-start | bytes 786436
  38.4 8.0 %collective-permute-start.3 = (bf16[512,256]{1,0:T(8,128)(2,1)S(1)}, bf16[512,256]{1,0:T(8,128)(2,1)S(1)}, u32[]{:S(2)}, u32[]{:S(2)}) collective-permute-start(bf16[512,256]{1,0:T(8,128)(2,1)S(1)} %collective-permute-done.2.refs_2_), channel_id=1, source_target_pairs={{0,1},{1,2},{2,3},{3,4},{4,5},{5,6},{6,7},{7,0},{8,9},{9,10},{10,1... | collective-permute-start | bytes 786440 | tf_op jit(solution)/shard_map/ppermute | solution.py:242
  38.8 7.8 %collective-permute-start.6 = (bf16[512,256]{1,0:T(8,128)(2,1)S(1)}, bf16[512,256]{1,0:T(8,128)(2,1)S(1)}, u32[]{:S(2)}, u32[]{:S(2)}) collective-permute-start(bf16[512,256]{1,0:T(8,128)(2,1)S(1)} %collective-permute-done.5.refs_6_), channel_id=1, source_target_pairs={{0,7},{1,0},{2,1},{3,2},{4,3},{5,4},{6,5},{7,6},{8,15},{9,8},{10,9... | collective-permute-start | bytes 786440 | tf_op jit(solution)/shard_map/ppermute | solution.py:244
  46.4 7.0 %collective-permute-start.4 = (bf16[512,256]{1,0:T(8,128)(2,1)S(1)}, bf16[512,256]{1,0:T(8,128)(2,1)S(1)}, u32[]{:S(2)}, u32[]{:S(2)}) collective-permute-start(bf16[512,256]{1,0:T(8,128)(2,1)S(1)} %collective-permute-done.3.refs_3_), channel_id=1, source_target_pairs={{0,1},{1,2},{2,3},{3,4},{4,5},{5,6},{6,7},{7,0},{8,9},{9,10},{10,1... | collective-permute-start | bytes 786440 | tf_op jit(solution)/shard_map/ppermute | solution.py:242
  62.2 32.8 %all-to-all-start.1 = ((bf16[8,128,512]{2,1,0:T(8,128)(2,1)}), bf16[8,128,512]{2,1,0:T(8,128)(2,1)S(1)}, u32[]{:S(2)}, u32[]{:S(2)}) async-start(bf16[8,128,512]{2,1,0:T(8,128)(2,1)} %bitcast.5), calls=%async_computation.1 | async-start | bytes 2097152 | tf_op jit(solution)/shard_map/all_to_all | solution.py:274
  67.8 70.3 %copy-start = (s32[2,4]{1,0:T(2,128)S(1)}, s32[2,4]{1,0:T(2,128)}, u32[]{:S(2)}) copy-start(s32[2,4]{1,0:T(2,128)} %constant.87.clone) | copy-start | bytes 100
  67.8 70.9 %copy-start.10 = (s32[4]{0:T(128)S(1)}, s32[4]{0:T(128)}, u32[]{:S(2)}) copy-start(s32[4]{0:T(128)} %constant.88.clone) | copy-start | bytes 52
  70.2 28.8 %collective-permute-start.7 = (bf16[8,512,256]{2,1,0:T(8,128)(2,1)}, bf16[8,512,256]{2,1,0:T(8,128)(2,1)S(1)}, u32[]{:S(2)}, u32[]{:S(2)}) collective-permute-start(bf16[8,512,256]{2,1,0:T(8,128)(2,1)} %join.1.refs_8_), channel_id=1, source_target_pairs={{0,16},{8,56},{16,32},{24,8},{32,48},{40,24},{48,0},{56,40},{1,17}... | collective-permute-start | bytes 6291464 | tf_op jit(solution)/shard_map/ppermute | solution.py:251
  95.0 52.0 %copy-start.1 = (bf16[8,128,512]{2,1,0:T(8,128)(2,1)}, bf16[8,128,512]{2,1,0:T(8,128)(2,1)S(1)}, u32[]{:S(2)}) copy-start(bf16[8,128,512]{2,1,0:T(8,128)(2,1)S(1)} %all-to-all-done.1.refs_0_) | copy-start | bytes 3145732
  95.0 15.3 %collective-permute-start.8 = (bf16[8,128,512]{2,1,0:T(8,128)(2,1)S(1)}, bf16[8,128,512]{2,1,0:T(8,128)(2,1)}, u32[]{:S(2)}, u32[]{:S(2)}) collective-permute-start(bf16[8,128,512]{2,1,0:T(8,128)(2,1)S(1)} %all-to-all-done.1.refs_0_), channel_id=1, source_target_pairs={{0,64},{8,200},{64,128},{72,8},{128,192},{136,72},{192,0},{200,136... | collective-permute-start | bytes 3145736 | tf_op jit(solution)/shard_map/ppermute | solution.py:251
  97.5 31.8 %collective-permute-start.15 = (bf16[8,512,256]{2,1,0:T(8,128)(2,1)}, bf16[8,512,256]{2,1,0:T(8,128)(2,1)S(1)}, u32[]{:S(2)}, u32[]{:S(2)}) collective-permute-start(bf16[8,512,256]{2,1,0:T(8,128)(2,1)} %join.1.refs_8_), channel_id=1, source_target_pairs={{0,48},{8,24},{16,0},{24,40},{32,16},{40,56},{48,32},{56,8},{1,49}... | collective-permute-start | bytes 6291464 | tf_op jit(solution)/shard_map/ppermute | solution.py:251
  99.0 48.1 %copy-start.11 = (bf16[8,512,256]{2,1,0:T(8,128)(2,1)}, bf16[8,512,256]{2,1,0:T(8,128)(2,1)S(1)}, u32[]{:S(2)}) copy-start(bf16[8,512,256]{2,1,0:T(8,128)(2,1)S(1)} %collective-permute-done.7.refs_9_) | copy-start | bytes 6291460
  110.3 22.9 %collective-permute-start.11 = (bf16[8,128,512]{2,1,0:T(8,128)(2,1)S(1)}, bf16[8,128,512]{2,1,0:T(8,128)(2,1)}, u32[]{:S(2)}, u32[]{:S(2)}) collective-permute-start(bf16[8,128,512]{2,1,0:T(8,128)(2,1)S(1)} %all-to-all-done.1.refs_0_), channel_id=1, source_target_pairs={{0,192},{8,72},{64,0},{72,136},{128,64},{136,200},{192,128},{200,8... | collective-permute-start | bytes 3145736 | tf_op jit(solution)/shard_map/ppermute | solution.py:251
  111.8 25.9 %collective-permute-start.13 = (bf16[8,128,512]{2,1,0:T(8,128)(2,1)}, bf16[8,128,512]{2,1,0:T(8,128)(2,1)}, u32[]{:S(2)}, u32[]{:S(2)}) collective-permute-start(bf16[8,128,512]{2,1,0:T(8,128)(2,1)} %collective-permute-done.8.refs_2_), channel_id=1, source_target_pairs={{0,64},{8,200},{64,128},{72,8},{128,192},{136,72},{192,0},{200,136... | collective-permute-start | bytes 3145736 | tf_op jit(solution)/shard_map/ppermute | solution.py:251
  113.0 34.1 %collective-permute-start.16 = (bf16[8,512,256]{2,1,0:T(8,128)(2,1)S(1)}, bf16[8,512,256]{2,1,0:T(8,128)(2,1)}, u32[]{:S(2)}, u32[]{:S(2)}) collective-permute-start(bf16[8,512,256]{2,1,0:T(8,128)(2,1)S(1)} %collective-permute-done.7.refs_9_), channel_id=1, source_target_pairs={{0,16},{8,56},{16,32},{24,8},{32,48},{40,24},{48,0},{56,40},{1,17}... | collective-permute-start | bytes 6291464 | tf_op jit(solution)/shard_map/ppermute | solution.py:251
  116.0 23.3 %collective-permute-start.9 = (bf16[8,128,512]{2,1,0:T(8,128)(2,1)S(1)}, bf16[8,128,512]{2,1,0:T(8,128)(2,1)}, u32[]{:S(2)}, u32[]{:S(2)}) collective-permute-start(bf16[8,128,512]{2,1,0:T(8,128)(2,1)S(1)} %all-to-all-done.1.refs_0_), channel_id=1, source_target_pairs={{0,8},{8,0},{1,9},{9,1},{2,10},{10,2},{3,11},{11,3},{4,12},{12,4},... | collective-permute-start | bytes 3145736 | tf_op jit(solution)/shard_map/ppermute | solution.py:280
  129.2 10.1 %collective-permute-start.10 = (bf16[8,128,512]{2,1,0:T(8,128)(2,1)}, bf16[8,128,512]{2,1,0:T(8,128)(2,1)}, u32[]{:S(2)}, u32[]{:S(2)}) collective-permute-start(bf16[8,128,512]{2,1,0:T(8,128)(2,1)} %collective-permute-done.8.refs_2_), channel_id=1, source_target_pairs={{0,8},{8,0},{1,9},{9,1},{2,10},{10,2},{3,11},{11,3},{4,12},{12,4},... | collective-permute-start | bytes 3145736 | tf_op jit(solution)/shard_map/ppermute | solution.py:280
  133.2 7.1 %collective-permute-start.12 = (bf16[8,128,512]{2,1,0:T(8,128)(2,1)}, bf16[8,128,512]{2,1,0:T(8,128)(2,1)}, u32[]{:S(2)}, u32[]{:S(2)}) collective-permute-start(bf16[8,128,512]{2,1,0:T(8,128)(2,1)} %collective-permute-done.11.refs_4_), channel_id=1, source_target_pairs={{0,8},{8,0},{1,9},{9,1},{2,10},{10,2},{3,11},{11,3},{4,12},{12,4},... | collective-permute-start | bytes 3145736 | tf_op jit(solution)/shard_map/ppermute | solution.py:280
  137.7 4.1 %collective-permute-start.14 = (bf16[8,128,512]{2,1,0:T(8,128)(2,1)}, bf16[8,128,512]{2,1,0:T(8,128)(2,1)}, u32[]{:S(2)}, u32[]{:S(2)}) collective-permute-start(bf16[8,128,512]{2,1,0:T(8,128)(2,1)} %collective-permute-done.13.refs_6_), channel_id=1, source_target_pairs={{0,8},{8,0},{1,9},{9,1},{2,10},{10,2},{3,11},{11,3},{4,12},{12,4},... | collective-permute-start | bytes 3145736 | tf_op jit(solution)/shard_map/ppermute | solution.py:280
  (8 other events, 118.7 us)
